TPU v7x, 32 devices: a whole 2x2x4 slice. The times are simulated.
32 devices in a mesh: dp: 4 (over y, x), row: 4 (over z), col: 2 (over core).
Axes of the slice: x: 2, y: 2, z: 4, core: 2. Of those that a mesh axis runs over, the one named last changes fastest.
Arguments:
- tokens: bfloat16 [8, 2048, 1024], P(('dp', 'col'), 'row'), may hold values from -6 to 6
- segments: int32 [8, 2048], P(('dp', 'col'), 'row'), may hold values from 0 to 2, as said below
- gain_attn: float32 [1024], replicated, may hold values from 0.1 to 1.9
- w_qkv: bfloat16 [3, 1024, 1024], P(None, 'col', 'row'), may hold values from -0.1875 to 0.1875
- w_attn_out: bfloat16 [1024, 1024], P('col', 'row'), may hold values from -0.75 to 0.75
- gain_mlp: float32 [1024], replicated, may hold values from 0.1 to 1.9
- w_in: bfloat16 [2, 2624, 1024], P(None, 'col', 'row'), may hold values from -0.1875 to 0.1875
- w_mlp: bfloat16 [2624, 1024], P('col', 'row'), may hold values from -0.125 to 0.125
- cotangent: bfloat16 [8, 2048, 1024], P(('dp', 'col'), 'row'), may hold values from -6 to 6
Outputs:
- output: bfloat16 [8, 2048, 1024], P(('dp', 'col'), 'row')
- grad_input: bfloat16 [8, 2048, 1024], P(('dp', 'col'), 'row')
- grad_w_qkv: float32 [3, 1024, 1024], P(None, 'col', 'row')
- grad_w_attn_out: float32 [1024, 1024], P('col', 'row')
- grad_w_in: float32 [2, 2624, 1024], P(None, 'col', 'row')
- grad_w_mlp: float32 [2624, 1024], P('col', 'row')
- grad_gain_attn: float32 [1024], P(('row', 'col'))
- grad_gain_mlp: float32 [1024], P(('row', 'col'))
Inputs may be any that keep to these rules, and one draw needn't show every extreme that they name: `segments`: along each sequence the ids never fall; a token attends only to tokens of its sequence with the same id.
All inputs are finite; a program needn't handle non-finite values.
Results may differ from a plain program's by a relative error of at most 0.015.
Values may be sent and summed in bfloat16 or wider, within the bound.
A program may use at most 384 MiB of HBM per device.

v0:
```python
import jax
import jax.numpy as jnp
from jax import lax
from jax.sharding import PartitionSpec as P

HEADS = 16
HEAD = 64


EPSILON = 1e-05
ROPE_BASE = 160000.0
MASKED = -1e30


def layer_norm(inputs, gain):
    average = jnp.mean(inputs, axis=-1, keepdims=True)
    centred = inputs - average
    variance = jnp.mean(centred * centred, axis=-1, keepdims=True)
    return centred * lax.rsqrt(variance + EPSILON) * gain


def rotary(positions):
    half_head = HEAD // 2
    frequency = jnp.power(ROPE_BASE, -2.0 * jnp.arange(half_head).astype(jnp.float32) / HEAD)
    angles = positions[:, None] * frequency[None, :]
    angles = jnp.concatenate([angles, angles], axis=-1)
    return (jnp.cos(angles), jnp.sin(angles))


def rope(inputs, cosine, sine_table):
    half_head = HEAD // 2
    turned = jnp.concatenate([-inputs[..., half_head:], inputs[..., :half_head]], axis=-1)
    return inputs * cosine[:, None, :] + turned * sine_table[:, None, :]


def geglu(act_in, gate_in):
    return jax.nn.gelu(act_in, approximate=False) * gate_in


def contract_rows(left_side, right_side):
    return lax.dot_general(
        left_side, right_side, (((0,), (0,)), ((), ())), preferred_element_type=jnp.float32
    )


def times_transpose(left_side, right_side):
    return lax.dot_general(
        left_side, right_side, (((1,), (1,)), ((), ())), preferred_element_type=jnp.float32
    )


def masked_scores(query_heads, key_rows, seg_query, seg_keys):
    seq_total = key_rows.shape[0]
    key_heads = key_rows.reshape(seq_total, HEADS, HEAD)
    raw_scores = jnp.einsum(
        "qhe,khe->hqk", query_heads, key_heads, preferred_element_type=jnp.float32
    )
    allowed = seg_query[None, :, None] == seg_keys[None, None, :]
    return jnp.where(allowed, raw_scores * HEAD ** (-0.5), MASKED)


def attend_forward(element):
    query_heads, key_rows, value_rows, seg_query, seg_keys = element
    logits = masked_scores(query_heads, key_rows, seg_query, seg_keys)
    highest = jnp.max(logits, axis=-1, keepdims=True)
    exponent = jnp.exp(logits - highest)
    summed = jnp.sum(exponent, axis=-1, keepdims=True)
    weights = (exponent / summed).astype(jnp.bfloat16)
    seq_total = value_rows.shape[0]
    value_heads = value_rows.reshape(seq_total, HEADS, HEAD)
    attended = jnp.einsum("hqk,khe->qhe", weights, value_heads, preferred_element_type=jnp.float32)
    return (attended.reshape(attended.shape[0], HEADS * HEAD), (highest + jnp.log(summed))[..., 0])


def score_grads(query_heads, key_rows, value_rows, seg_query, seg_keys, log_total, grad_heads):
    logits = masked_scores(query_heads, key_rows, seg_query, seg_keys)
    probs = jnp.exp(logits - log_total[..., None])
    seq_total = value_rows.shape[0]
    value_heads = value_rows.reshape(seq_total, HEADS, HEAD)
    grad_probs = jnp.einsum(
        "qhe,khe->hqk", grad_heads, value_heads, preferred_element_type=jnp.float32
    )
    return (probs, grad_probs)


def attend_backward(element):
    query_heads, key_rows, value_rows, seg_query, seg_keys, log_total, grad_heads = element
    probs, grad_probs = score_grads(
        query_heads, key_rows, value_rows, seg_query, seg_keys, log_total, grad_heads
    )
    inner = jnp.sum(grad_probs * probs, axis=-1, keepdims=True)
    grad_scores = (probs * (grad_probs - inner) * HEAD ** (-0.5)).astype(jnp.bfloat16)
    seq_total = key_rows.shape[0]
    key_heads = key_rows.reshape(seq_total, HEADS, HEAD)
    grad_query = jnp.einsum(
        "hqk,khe->qhe", grad_scores, key_heads, preferred_element_type=jnp.float32
    )
    grad_key = jnp.einsum(
        "hqk,qhe->khe", grad_scores, query_heads, preferred_element_type=jnp.float32
    )
    grad_value = jnp.einsum(
        "hqk,qhe->khe", probs.astype(jnp.bfloat16), grad_heads, preferred_element_type=jnp.float32
    )
    return (
        grad_query,
        grad_key.reshape(seq_total, HEADS * HEAD),
        grad_value.reshape(seq_total, HEADS * HEAD),
    )


def body(tokens, segments, gain_attn, w_qkv, w_attn_out, gain_mlp, w_in, w_mlp, cotangent):
    seq_count, local_rows, width = tokens.shape
    flat_rows = seq_count * local_rows
    qkv_cols, out_cols = (
        lax.all_gather(w_qkv, "col", axis=1, tiled=True),
        lax.all_gather(w_attn_out, "col", axis=0, tiled=True),
    )
    inner_cols, mlp_cols = (w_in, w_mlp)
    qkv_full, out_full, inner_full, mlp_full = (
        lax.all_gather(qkv_cols, "row", axis=2, tiled=True),
        lax.all_gather(out_cols, "row", axis=1, tiled=True),
        lax.all_gather(inner_cols, "row", axis=2, tiled=True),
        lax.all_gather(mlp_cols, "row", axis=1, tiled=True),
    )
    qkv_matrix = qkv_full.reshape(3 * width, width)
    hidden_units = inner_full.shape[1]
    inner_matrix = inner_full.reshape(2 * hidden_units, width)
    inputs = tokens.astype(jnp.float32).reshape(flat_rows, width)
    norm_one = layer_norm(inputs, gain_attn).astype(jnp.bfloat16)
    projected = times_transpose(norm_one, qkv_matrix).reshape(seq_count, local_rows, 3, HEADS, HEAD)
    positions = (
        lax.axis_index("row") * local_rows + jnp.arange(local_rows, dtype=jnp.int32)
    ).astype(jnp.float32)
    cosine, sine_table = rotary(positions)

    def turn(heads_in):
        return rope(heads_in, cosine, sine_table)

    query_heads = turn(projected[:, :, 0]).astype(jnp.bfloat16)
    key_rows = turn(projected[:, :, 1]).astype(jnp.bfloat16).reshape(seq_count, local_rows, width)
    value_rows = projected[:, :, 2].astype(jnp.bfloat16).reshape(seq_count, local_rows, width)
    key_all, value_all, seg_all = (
        lax.all_gather(key_rows, "row", axis=1, tiled=True),
        lax.all_gather(value_rows, "row", axis=1, tiled=True),
        lax.all_gather(segments, "row", axis=1, tiled=True),
    )
    attended, log_total = lax.map(
        attend_forward, (query_heads, key_all, value_all, segments, seg_all)
    )
    mixed = attended.astype(jnp.bfloat16).reshape(flat_rows, width)
    residual = inputs + times_transpose(mixed, out_full)
    norm_two = layer_norm(residual, gain_mlp).astype(jnp.bfloat16)
    cot_flat = cotangent.reshape(flat_rows, width)
    norm_all, cot_all = (
        lax.all_gather(norm_two.reshape(seq_count, local_rows, width), "col", axis=0, tiled=True),
        lax.all_gather(cotangent, "col", axis=0, tiled=True),
    )
    mlp_inputs = norm_all.reshape(-1, width)
    mlp_cot = cot_all.reshape(-1, width)
    lifted = times_transpose(mlp_inputs, inner_matrix).reshape(-1, 2, hidden_units)
    gated = geglu(lifted[:, 0], lifted[:, 1]).astype(jnp.bfloat16)
    block = gated
    mlp_out = (
        lax.psum_scatter(
            jnp.dot(block, mlp_full, preferred_element_type=jnp.float32)
            .reshape(seq_count * lax.axis_size("col"), local_rows, width)
            .astype(jnp.bfloat16),
            "col",
            scatter_dimension=0,
            tiled=True,
        )
        .astype(jnp.float32)
        .reshape(flat_rows, width)
    )
    output = (residual + mlp_out).astype(jnp.bfloat16).reshape(seq_count, local_rows, width)
    grad_gated = times_transpose(mlp_cot, mlp_full)
    grad_w_mlp = contract_rows(gated, mlp_cot)
    geglu_back = jax.vjp(geglu, lifted[:, 0], lifted[:, 1])[1]
    grad_act, grad_gate = geglu_back(grad_gated)
    grad_lifted = (
        jnp.stack([grad_act, grad_gate], axis=1).astype(jnp.bfloat16).reshape(-1, 2 * hidden_units)
    )
    grad_inner = contract_rows(grad_lifted, mlp_inputs).reshape(2, hidden_units, width)
    block = grad_lifted
    grad_norm_two = lax.psum_scatter(
        jnp.dot(block, inner_matrix, preferred_element_type=jnp.float32).reshape(
            lax.axis_size("col") * seq_count, local_rows, width
        ),
        "col",
        scatter_dimension=0,
        tiled=True,
    ).reshape(flat_rows, width)
    second_back = jax.vjp(layer_norm, residual, gain_mlp)[1]
    grad_resid_part, grad_gain_mlp = second_back(grad_norm_two)
    grad_residual = cot_flat.astype(jnp.float32) + grad_resid_part
    grad_resid_low = grad_residual.astype(jnp.bfloat16)
    grad_w_out = contract_rows(grad_resid_low, mixed)
    grad_mixed = (
        jnp.dot(grad_resid_low, out_full, preferred_element_type=jnp.float32)
        .astype(jnp.bfloat16)
        .reshape(seq_count, local_rows, HEADS, HEAD)
    )
    grad_queries, key_terms, value_terms = lax.map(
        attend_backward, (query_heads, key_all, value_all, segments, seg_all, log_total, grad_mixed)
    )
    grad_keys, grad_values = (
        lax.psum_scatter(key_terms, "row", scatter_dimension=1, tiled=True),
        lax.psum_scatter(value_terms, "row", scatter_dimension=1, tiled=True),
    )
    turn_back = jax.vjp(turn, projected[:, :, 0])[1]
    grad_query_raw = turn_back(grad_queries)[0]
    grad_key_raw = turn_back(grad_keys.reshape(seq_count, local_rows, HEADS, HEAD))[0]
    grad_value_raw = grad_values.reshape(seq_count, local_rows, HEADS, HEAD)
    grad_projected = (
        jnp.stack([grad_query_raw, grad_key_raw, grad_value_raw], axis=2)
        .astype(jnp.bfloat16)
        .reshape(flat_rows, 3 * width)
    )
    grad_w_qkv = contract_rows(grad_projected, norm_one).reshape(3, width, width)
    grad_norm_one = jnp.dot(grad_projected, qkv_matrix, preferred_element_type=jnp.float32)
    first_back = jax.vjp(layer_norm, inputs, gain_attn)[1]
    grad_in_part, grad_gain_attn = first_back(grad_norm_one)
    grad_input = (
        (grad_residual + grad_in_part).astype(jnp.bfloat16).reshape(seq_count, local_rows, width)
    )
    row_sums = (
        lax.psum_scatter(grad_w_qkv, "row", scatter_dimension=2, tiled=True),
        lax.psum_scatter(grad_w_out, "row", scatter_dimension=1, tiled=True),
        lax.psum_scatter(grad_inner, "row", scatter_dimension=2, tiled=True),
        lax.psum_scatter(grad_w_mlp, "row", scatter_dimension=1, tiled=True),
        lax.psum_scatter(grad_gain_attn, "row", scatter_dimension=0, tiled=True),
        lax.psum_scatter(grad_gain_mlp, "row", scatter_dimension=0, tiled=True),
    )
    qkv_part, out_part, gain_one, gain_two = (
        lax.psum_scatter(row_sums[0], "col", scatter_dimension=1, tiled=True),
        lax.psum_scatter(row_sums[1], "col", scatter_dimension=0, tiled=True),
        lax.psum_scatter(row_sums[4], "col", scatter_dimension=0, tiled=True),
        lax.psum_scatter(row_sums[5], "col", scatter_dimension=0, tiled=True),
    )
    inner_part, mlp_part = (row_sums[2], row_sums[3])
    totals = lax.psum((qkv_part, out_part, inner_part, mlp_part, gain_one, gain_two), "dp")
    return (output, grad_input, totals[0], totals[1], totals[2], totals[3], totals[4], totals[5])


def solution(mesh):
    return jax.shard_map(
        body,
        mesh=mesh,
        in_specs=(
            P(("dp", "col"), "row", None),
            P(("dp", "col"), "row"),
            P(),
            P(None, "col", "row"),
            P("col", "row"),
            P(),
            P(None, "col", "row"),
            P("col", "row"),
            P(("dp", "col"), "row", None),
        ),
        out_specs=(
            P(("dp", "col"), "row", None),
            P(("dp", "col"), "row", None),
            P(None, "col", "row"),
            P("col", "row"),
            P(None, "col", "row"),
            P("col", "row"),
            P(("row", "col")),
            P(("row", "col")),
        ),
        check_vma=False,
    )
```

profile of v0, /device:TPU:0, one launch (start us, length us, event | category | flops | bytes accessed | tf_op | source)
XLA Modules:
  0.0 1838.8 jit_solution(7466380088588866193)
XLA Ops:
  7.9 14.1 all-gather.11.cloned.1.call-done
  24.1 1.6 fusion.79
  25.7 114.0 %all-gather.13.cloned.1.call-done = bf16[3,1024,1024]{2,1,0:T(8,128)(2,1)} async-done(((bf16[3,1024,256]{2,1,0:T(8,128)(2,1)}), bf16[3,1024,1024]{2,1,0:T(8,128)(2,1)}) %all-gather.13.cloned.1.call-update) | async-done | bytes 6291472 | tf_op jit(solution)/shard_map/all_gather | solution.py:120
  139.7 6.7 convolution_bitcast_fusion
  147.4 1.7 copy-done.8
  149.3 1.6 fusion.97
  151.0 2.7 slice.78
  153.8 2.3 all_gather.41
  158.3 12.0 all_gather.38
  171.3 2.3 fusion.87
  173.6 56.6 %all-gather.17.cloned.1.call-done = bf16[1,2048,1024]{1,2,0:T(8,128)(2,1)} async-done(((bf16[1,512,1024]{1,2,0:T(8,128)(2,1)}), bf16[1,2048,1024]{1,2,0:T(8,128)(2,1)}) %all-gather.17.cloned.1.call-update) | async-done | bytes 4194320 | tf_op jit(solution)/shard_map/all_gather | solution.py:143
  230.2 27.3 %fusion.3 = (f32[16,512]{1,0:T(8,128)S(1)}, f32[16,512,2048]{2,1,0:T(8,128)}) fusion(pred[512,2048]{1,0:T(8,128)(4,1)S(1)} %broadcast_compare_fusion, bf16[512,16,64]{0,2,1:T(8,128)(2,1)S(1)} %fusion.87, bf16[2048,16,64]{0,2,1:T(8,128)(2,1)} %bitcast.274), kind=kOutput, calls=%fused_computation.9 | convolution fusion | flops 2197807104 | bytes 73433088 | tf_op jit(solution)/shard_map/while/body/eval_jaxpr/qhe,khe->hqk/dot_general | solution.py:55
  257.4 21.8 %fusion.2 = f32[16,512]{1,0:T(8,128)S(1)} fusion(f32[16,512,2048]{2,1,0:T(8,128)} %get-tuple-element.103, f32[16,512]{1,0:T(8,128)S(1)} %get-tuple-element.102, pred[512,2048]{1,0:T(8,128)(4,1)S(1)} %broadcast_compare_fusion), kind=kLoop, calls=%fused_computation.8 | loop fusion | flops 67100672 | bytes 68222976 | tf_op jit(solution)/shard_map/while/body/eval_jaxpr/reduce_sum | solution.py:67
  279.2 32.3 %all-gather.15.cloned.1.call-done = bf16[1,2048,1024]{1,2,0:T(8,128)(2,1)} async-done(((bf16[1,512,1024]{1,2,0:T(8,128)(2,1)}), bf16[1,2048,1024]{1,2,0:T(8,128)(2,1)}) %all-gather.15.cloned.1.call-update) | async-done | bytes 4194320 | tf_op jit(solution)/shard_map/all_gather | solution.py:144
  311.5 28.3 %fusion.103 = bf16[16,64,512]{2,1,0:T(8,128)(2,1)} fusion(bf16[2048,16,64]{0,2,1:T(8,128)(2,1)} %bitcast.276, f32[16,512,2048]{2,1,0:T(8,128)} %get-tuple-element.103, f32[16,512]{1,0:T(8,128)S(1)} %fusion.2, f32[16,512]{1,0:T(8,128)S(1)} %get-tuple-element.102, pred[512,2048]{1,0:T(8,128)(4,1)S(1)} %broadcast_compare_fusion), kind=kOutput, calls=%fused_computation.151 | convolution fusion | flops 2231894016 | bytes 73465856 | tf_op jit(solution)/shard_map/while/body/eval_jaxpr/hqk,khe->qhe/dot_general | solution.py:71
  339.8 17.9 all-gather.19.cloned.1.call-done
  357.7 3.6 fusion.194
  363.1 4.9 all-gather.25.cloned.1.call-done
  368.0 58.7 %all-gather.23.cloned.1.call-done = bf16[1312,1024]{1,0:T(8,128)(2,1)} async-done(((bf16[1312,256]{1,0:T(8,128)(2,1)}), bf16[1312,1024]{1,0:T(8,128)(2,1)}) %all-gather.23.cloned.1.call-update) | async-done | bytes 2686992 | tf_op jit(solution)/shard_map/all_gather | solution.py:123
  426.7 7.9 fusion.195
  434.5 91.8 %all-gather.21.cloned.1.call-done = bf16[2,1312,1024]{2,1,0:T(8,128)(2,1)} async-done(((bf16[2,1312,256]{2,1,0:T(8,128)(2,1)}), bf16[2,1312,1024]{2,1,0:T(8,128)(2,1)}) %all-gather.21.cloned.1.call-update) | async-done | bytes 5373968 | tf_op jit(solution)/shard_map/all_gather | solution.py:122
  526.3 10.9 all-gather.27.cloned.1.call-done
  537.2 8.8 fusion.94
  546.0 14.2 fusion.38
  560.2 7.8 fusion.40
  568.0 5.4 maximum_convert_fusion
  573.4 13.0 convert_element_type.168
  586.4 11.0 fusion.41
  597.5 12.0 negate_multiply_fusion
  609.5 8.7 mul.368
  618.2 8.2 squeeze.56
  626.4 8.3 mul.366
  634.7 19.5 %fusion.98 = bf16[2,512,1024]{2,1,0:T(8,128)(2,1)} fusion(bf16[1312,1024]{1,0:T(8,128)(2,1)} %all-gather.23.cloned.1.call-done, f32[2,512,1312]{1,0,2:T(2,128)} %squeeze.56, f32[2,512,1312]{1,0,2:T(2,128)} %mul.366, f32[2,512,1312]{1,0,2:T(2,128)} %mul.368), kind=kOutput, calls=%fused_computation.149 | convolution fusion | flops 2837151744 | bytes 20905984 | tf_op jit(solution)/shard_map/dot_general | solution.py:165
  654.5 2.9 fusion.92
  657.4 7.7 reduce-scatter.11.cloned.1.call-done
  665.1 3.8 fusion.189
  673.3 25.6 %fusion.196 = f32[16,512,2048]{2,1,0:T(8,128)} fusion(bf16[512,16,64]{0,2,1:T(8,128)(2,1)S(1)} %bitcast.278, bf16[2048,16,64]{0,2,1:T(8,128)(2,1)} %bitcast.277), kind=kOutput, calls=%fused_computation.257 | convolution fusion | flops 2147483648 | bytes 72351744 | tf_op jit(solution)/shard_map/while/body/eval_jaxpr/qhe,khe->hqk/dot_general | solution.py:80
  698.9 84.6 %fusion.16 = f32[16,64,2048]{2,1,0:T(8,128)} fusion(bf16[512,16,64]{0,2,1:T(8,128)(2,1)S(1)} %copy-done.12, f32[16,512,2048]{2,1,0:T(8,128)} %fusion.196, f32[16,512,2048]{2,1,0:T(8,128)} %get-tuple-element.103, f32[16,512]{1,0:T(8,128)S(1)} %log_add_fusion, pred[512,2048]{1,0:T(8,128)(4,1)S(1)} %copy-done.2), kind=kOutput, calls=%fused_computation.18 | convolution fusion | flops 2332043264 | bytes 144736256 | tf_op jit(solution)/shard_map/while/body/eval_jaxpr/hqk,qhe->khe/dot_general | solution.py:98
  783.5 30.1 %fusion.10 = f32[16,64,2048]{2,1,0:T(8,128)} fusion(bf16[512,16,64]{0,2,1:T(8,128)(2,1)S(1)} %bitcast.279, f32[16,512,2048]{2,1,0:T(8,128)} %get-tuple-element.103, f32[16,512]{1,0:T(8,128)S(1)} %log_add_fusion, pred[512,2048]{1,0:T(8,128)(4,1)S(1)} %copy-done.2), kind=kOutput, calls=%fused_computation.14 | convolution fusion | flops 2214592512 | bytes 77627392 | tf_op jit(solution)/shard_map/while/body/eval_jaxpr/hqk,qhe->khe/dot_general | solution.py:101
  815.2 3.3 fusion.197
  818.8 83.9 %fusion.19 = f32[16,64,512]{2,1,0:T(8,128)S(1)} fusion(bf16[2048,16,64]{0,2,1:T(8,128)(2,1)} %bitcast.275, f32[16,512,2048]{2,1,0:T(8,128)} %fusion.196, f32[16,512,2048]{2,1,0:T(8,128)} %get-tuple-element.103, f32[16,512]{1,0:T(8,128)S(1)} %log_add_fusion, pred[512,2048]{1,0:T(8,128)(4,1)S(1)} %copy-done.2), kind=kOutput, calls=%fused_computation.19 | convolution fusion | flops 2332043264 | bytes 141590528 | tf_op jit(solution)/shard_map/while/body/eval_jaxpr/hqk,khe->qhe/dot_general | solution.py:95
  904.5 24.8 %reduce-scatter.15.cloned.1.call-done = f32[1,512,1024]{1,2,0:T(8,128)} async-done(((f32[1,2048,1024]{1,2,0:T(8,128)}), f32[1,512,1024]{1,2,0:T(8,128)}) %reduce-scatter.15.cloned.1.call-update) | async-done | bytes 2097168 | tf_op jit(solution)/shard_map/reduce_scatter | solution.py:207
  929.3 2.0 broadcast_multiply_fusion
  932.1 2.1 fusion.90
  934.3 142.6 %reduce-scatter.17.cloned.1.call-done = f32[1,512,1024]{1,2,0:T(8,128)} async-done(((f32[1,2048,1024]{1,2,0:T(8,128)}), f32[1,512,1024]{1,2,0:T(8,128)}) %reduce-scatter.17.cloned.1.call-update) | async-done | bytes 2097168 | tf_op jit(solution)/shard_map/reduce_scatter | solution.py:208
  1076.9 2.3 maximum_convert_fusion.1
  1079.2 1.7 copy-done.19
  1080.9 6.7 fusion.109
  1089.3 16.9 fusion.67
  1106.5 50.1 %reduce-scatter.23.cloned.1.call-done = f32[1024,256]{1,0:T(8,128)} async-done(((f32[1024,1024]{1,0:T(8,128)}), f32[1024,256]{1,0:T(8,128)}) %reduce-scatter.23.cloned.1.call-update) | async-done | bytes 1048592 | tf_op jit(solution)/shard_map/reduce_scatter | solution.py:228
  1156.7 11.0 fusion.30
  1167.8 203.5 %reduce-scatter.19.cloned.1.call-done = f32[3,1024,256]{2,1,0:T(8,128)} async-done(((f32[3,1024,1024]{2,1,0:T(8,128)}), f32[3,1024,256]{2,1,0:T(8,128)}) %reduce-scatter.19.cloned.1.call-update) | async-done | bytes 3145744 | tf_op jit(solution)/shard_map/reduce_scatter | solution.py:227
  1371.4 99.2 %reduce-scatter.29.cloned.1.call-done = f32[1312,256]{1,0:T(8,128)} async-done(((f32[1312,1024]{1,0:T(8,128)}), f32[1312,256]{1,0:T(8,128)}) %reduce-scatter.29.cloned.1.call-update) | async-done | bytes 1343504 | tf_op jit(solution)/shard_map/reduce_scatter | solution.py:230
  1470.5 11.2 reduce-scatter.25.cloned.1.call-done
  1481.8 185.7 %reduce-scatter.27.cloned.1.call-done = f32[2,1312,256]{2,1,0:T(8,128)} async-done(((f32[2,1312,1024]{2,1,0:T(8,128)}), f32[2,1312,256]{2,1,0:T(8,128)}) %reduce-scatter.27.cloned.1.call-update) | async-done | bytes 2686992 | tf_op jit(solution)/shard_map/reduce_scatter | solution.py:229
  1667.4 14.2 reduce-scatter.21.cloned.1.call-done
  1684.2 6.8 fusion.80
  1693.4 12.1 all-reduce.8
  1705.6 2.4 all-reduce.11
  1708.2 10.6 all-reduce.9
  1718.8 3.2 fusion.105
  1722.0 102.2 %all-reduce.14.cloned.1.call-done = (f32[3,512,256]{2,1,0:T(8,128)}, f32[512,256]{1,0:T(8,128)}, f32[2,1312,256]{2,1,0:T(8,128)}, f32[1312,256]{1,0:T(8,128)}) async-done(((f32[3,512,256]{2,1,0:T(8,128)}, f32[512,256]{1,0:T(8,128)}, f32[2,1312,256]{2,1,0:T(8,128)}, f32[1312,256]{1,0:T(8,128)}), (f32[3,512,256]{2,1,0:T(8,128)}, f32[512,256]{1,0:T(8,128)}, f32[2,1312,256]{2,1,0:T(8,128)}, ...) | async-done | bytes 6127632 | tf_op jit(solution)/shard_map/psum | solution.py:241
  1824.2 2.8 copy.64
  1827.0 1.9 copy.65
  (161 shorter events, 26.4 us)
Async XLA Ops:
  7.2 14.9 all-gather.11.cloned.1.call-start
  7.9 131.8 %all-gather.13.cloned.1.call-start = ((), (), s32[]{:S(2)}) async-start(), calls=%async_computation.11 | async-start | bytes 7864320 | tf_op jit(solution)/shard_map/all_gather | solution.py:120
  22.1 208.1 %all-gather.17.cloned.1.call-start = ((), (), s32[]{:S(2)}) async-start(), calls=%async_computation.13 | async-start | bytes 5242880 | tf_op jit(solution)/shard_map/all_gather | solution.py:143
  22.5 148.7 %copy-start.15 = (f32[512,64]{0,1:T(8,128)}, f32[512,64]{0,1:T(8,128)S(1)}, u32[]{:S(2)}) copy-start(f32[512,64]{0,1:T(8,128)S(1)} %get-tuple-element.101) | copy-start | bytes 393220
  22.5 148.7 %copy-start.17 = (f32[512,64]{0,1:T(8,128)}, f32[512,64]{0,1:T(8,128)S(1)}, u32[]{:S(2)}) copy-start(f32[512,64]{0,1:T(8,128)S(1)} %get-tuple-element.100) | copy-start | bytes 393220
  24.1 122.3 %copy-start.26 = (f32[512]{0:T(512)}, f32[512]{0:T(512)S(1)}, u32[]{:S(2)}) copy-start(f32[512]{0:T(512)S(1)} %broadcast_multiply_fusion.3) | copy-start | bytes 6148
  25.7 120.7 %copy-start.32 = (f32[512]{0:T(512)}, f32[512]{0:T(512)S(1)}, u32[]{:S(2)}) copy-start(f32[512]{0:T(512)S(1)} %fusion.79) | copy-start | bytes 6148
  25.7 120.7 %copy-start.28 = (f32[512]{0:T(512)}, f32[512]{0:T(512)S(1)}, u32[]{:S(2)}) copy-start(f32[512]{0:T(512)S(1)} %fusion.113) | copy-start | bytes 6148
  146.4 2.7 copy-start.8
  149.3 4.5 copy-start.24
  150.9 7.3 copy-start.36
  151.0 160.6 %all-gather.15.cloned.1.call-start = ((), (), s32[]{:S(2)}) async-start(), calls=%async_computation.12 | async-start | bytes 5242880 | tf_op jit(solution)/shard_map/all_gather | solution.py:144
  153.8 204.0 %all-gather.19.cloned.1.call-start = ((), (), s32[]{:S(2)}) async-start(), calls=%async_computation.14 | async-start | bytes 2621440 | tf_op jit(solution)/shard_map/all_gather | solution.py:121
  156.2 211.8 %all-gather.25.cloned.1.call-start = ((), (), s32[]{:S(2)}) async-start(), calls=%async_computation.18 | async-start | bytes 3145728 | tf_op jit(solution)/shard_map/all_gather | solution.py:156
  156.7 269.9 %all-gather.23.cloned.1.call-start = ((), (), s32[]{:S(2)}) async-start(), calls=%async_computation.16 | async-start | bytes 3358720 | tf_op jit(solution)/shard_map/all_gather | solution.py:123
  157.5 368.8 %all-gather.21.cloned.1.call-start = ((), (), s32[]{:S(2)}) async-start(), calls=%async_computation.15 | async-start | bytes 6717440 | tf_op jit(solution)/shard_map/all_gather | solution.py:122
  158.2 379.0 %all-gather.27.cloned.1.call-start = ((), (), s32[]{:S(2)}) async-start(), calls=%async_computation.28 | async-start | bytes 3145728 | tf_op jit(solution)/shard_map/all_gather | solution.py:155
  171.0 140.6 %copy-start.1 = (pred[512,2048]{1,0:T(8,128)(4,1)}, pred[512,2048]{1,0:T(8,128)(4,1)S(1)}, u32[]{:S(2)}) copy-start(pred[512,2048]{1,0:T(8,128)(4,1)S(1)} %broadcast_compare_fusion) | copy-start | bytes 3145732
  173.6 83.9 %copy-start.11 = (bf16[512,16,64]{0,2,1:T(8,128)(2,1)}, bf16[512,16,64]{0,2,1:T(8,128)(2,1)S(1)}, u32[]{:S(2)}) copy-start(bf16[512,16,64]{0,2,1:T(8,128)(2,1)S(1)} %fusion.87) | copy-start | bytes 3145732
  357.7 3.9 copy-start.25
  363.0 291.4 %reduce-scatter.13.cloned.1.call-start = ((), (), s32[]{:S(2)}) async-start(), calls=%async_computation.19 | async-start | bytes 6291456 | tf_op jit(solution)/shard_map/reduce_scatter | solution.py:185
  537.2 8.8 copy-start.3
  546.0 14.2 copy-start
  597.5 67.6 %reduce-scatter.11.cloned.1.call-start = ((), (), s32[]{:S(2)}) async-start(), calls=%async_computation.17 | async-start | bytes 3145728 | tf_op jit(solution)/shard_map/reduce_scatter | solution.py:164
  654.2 275.1 %reduce-scatter.15.cloned.1.call-start = ((), (), s32[]{:S(2)}) async-start(), calls=%async_computation.20 | async-start | bytes 10485760 | tf_op jit(solution)/shard_map/reduce_scatter | solution.py:207
  654.4 15.7 copy-start.7
  665.1 6.4 copy-start.39
  668.8 1.3 copy-start.4
  668.8 1.6 copy-start.30
  670.5 1.0 copy-start.22
  673.3 25.6 %copy-start.2 = (pred[512,2048]{1,0:T(8,128)(4,1)S(1)}, pred[512,2048]{1,0:T(8,128)(4,1)}, u32[]{:S(2)}) copy-start(pred[512,2048]{1,0:T(8,128)(4,1)} %copy-done.1) | copy-start | bytes 3145732
  673.3 25.6 %copy-start.12 = (bf16[512,16,64]{0,2,1:T(8,128)(2,1)S(1)}, bf16[512,16,64]{0,2,1:T(8,128)(2,1)}, u32[]{:S(2)}) copy-start(bf16[512,16,64]{0,2,1:T(8,128)(2,1)} %copy-done.11) | copy-start | bytes 3145732
  783.5 293.4 %reduce-scatter.17.cloned.1.call-start = ((), (), s32[]{:S(2)}) async-start(), calls=%async_computation.21 | async-start | bytes 10485760 | tf_op jit(solution)/shard_map/reduce_scatter | solution.py:208
  813.7 1.2 copy-start.23
  813.7 1.5 copy-start.40
  813.7 342.9 %reduce-scatter.23.cloned.1.call-start = ((), (), s32[]{:S(2)}) async-start(), calls=%async_computation.24 | async-start | bytes 5242880 | tf_op jit(solution)/shard_map/reduce_scatter | solution.py:228
  818.6 84.1 %copy-start.16 = (f32[512,64]{0,1:T(8,128)S(1)}, f32[512,64]{0,1:T(8,128)}, u32[]{:S(2)}) copy-start(f32[512,64]{0,1:T(8,128)} %copy-done.15) | copy-start | bytes 393220
  818.6 552.7 %reduce-scatter.19.cloned.1.call-start = ((), (), s32[]{:S(2)}) async-start(), calls=%async_computation.22 | async-start | bytes 15728640 | tf_op jit(solution)/shard_map/reduce_scatter | solution.py:227
  903.0 28.6 %copy-start.18 = (f32[512,64]{0,1:T(8,128)S(1)}, f32[512,64]{0,1:T(8,128)}, u32[]{:S(2)}) copy-start(f32[512,64]{0,1:T(8,128)} %copy-done.17) | copy-start | bytes 393220
  929.3 2.2 copy-start.10
  929.3 2.5 copy-start.13
  929.3 2.8 copy-start.14
  934.2 146.7 %copy-start.6 = (bf16[1,512,1024]{2,1,0:T(8,128)(2,1)S(1)}, bf16[1,512,1024]{2,1,0:T(8,128)(2,1)}, u32[]{:S(2)}) copy-start(bf16[1,512,1024]{2,1,0:T(8,128)(2,1)} %param.9) | copy-start | bytes 3145732
  934.3 146.7 %copy-start.27 = (f32[512]{0:T(512)S(1)}, f32[512]{0:T(512)}, u32[]{:S(2)}) copy-start(f32[512]{0:T(512)} %copy-done.26) | copy-start | bytes 6148
  934.3 146.7 %copy-start.29 = (f32[512]{0:T(512)S(1)}, f32[512]{0:T(512)}, u32[]{:S(2)}) copy-start(f32[512]{0:T(512)} %copy-done.28) | copy-start | bytes 6148
  934.3 146.7 %copy-start.34 = (f32[1024]{0:T(1024)S(1)}, f32[1024]{0:T(1024)}, u32[]{:S(2)}) copy-start(f32[1024]{0:T(1024)} %param.11) | copy-start | bytes 12292
  1079.2 1.7 copy-start.19
  1087.7 1.6 copy-start.37
  1087.7 382.8 %reduce-scatter.29.cloned.1.call-start = ((), (), s32[]{:S(2)}) async-start(), calls=%async_computation.27 | async-start | bytes 6717440 | tf_op jit(solution)/shard_map/reduce_scatter | solution.py:230
  1106.2 50.5 %copy-start.38 = (bf16[1024,1024]{1,0:T(8,128)(2,1)S(1)}, bf16[1024,1024]{1,0:T(8,128)(2,1)}, u32[]{:S(2)}) copy-start(bf16[1024,1024]{1,0:T(8,128)(2,1)} %all-gather.27.cloned.1.call-done) | copy-start | bytes 6291460
  1106.2 375.6 %reduce-scatter.25.cloned.1.call-start = ((), (), s32[]{:S(2)}) async-start(), calls=%async_computation.25 | async-start | bytes 1572864 | tf_op jit(solution)/shard_map/reduce_scatter | solution.py:236
  1156.6 510.8 %reduce-scatter.27.cloned.1.call-start = ((), (), s32[]{:S(2)}) async-start(), calls=%async_computation.26 | async-start | bytes 13434880 | tf_op jit(solution)/shard_map/reduce_scatter | solution.py:229
  1167.7 514.0 %copy-start.42 = (u32[32]{0:T(128)S(1)}, u32[32]{0:T(128)}, u32[]{:S(2)}) copy-start(u32[32]{0:T(128)} %constant.165) | copy-start | bytes 388
  1167.7 514.5 %copy-start.41 = (u32[32]{0:T(128)S(1)}, u32[32]{0:T(128)}, u32[]{:S(2)}) copy-start(u32[32]{0:T(128)} %constant.161) | copy-start | bytes 388
  1167.7 513.9 %reduce-scatter.21.cloned.1.call-start = ((), (), s32[]{:S(2)}) async-start(), calls=%async_computation.23 | async-start | bytes 4718592 | tf_op jit(solution)/shard_map/reduce_scatter | solution.py:235
  1371.3 452.9 %all-reduce.14.cloned.1.call-start = ((), (), s32[]{:S(2)}) async-start(), calls=%async_computation.29 | async-start | bytes 12255232 | tf_op jit(solution)/shard_map/psum | solution.py:241
  1684.2 6.9 copy-start.33
  1684.2 9.2 copy-start.35
  1684.2 34.6 %copy-start.5 = (f32[512,1024]{1,0:T(8,128)S(1)}, f32[512,1024]{1,0:T(8,128)}, u32[]{:S(2)}) copy-start(f32[512,1024]{1,0:T(8,128)} %copy-done.4) | copy-start | bytes 6291460
  1684.2 34.6 %copy-start.31 = (f32[512]{0:T(512)S(1)}, f32[512]{0:T(512)}, u32[]{:S(2)}) copy-start(f32[512]{0:T(512)} %copy-done.30) | copy-start | bytes 6148
  1691.0 1.3 copy-start.9
  1824.2 4.7 copy-start.20
  1824.2 6.2 copy-start.21
Sparse Core Ops, SparseCore 0:
  9.5 12.4 all-gather.10
  23.6 116.0 all-gather.12
  151.1 79.0 all-gather.16
  232.2 79.3 all-gather.14
  312.9 44.7 all-gather.18
  359.1 8.7 all-gather.24
  369.5 57.0 all-gather.22
  428.2 98.0 all-gather.20
  528.4 8.7 all-gather.26
  597.6 13.2 reduce-scatter.12
  654.3 10.7 reduce-scatter.10
  783.6 145.6 reduce-scatter.14
  931.7 145.1 reduce-scatter.16
  1079.1 77.4 reduce-scatter.22
  1158.9 212.3 reduce-scatter.18
  1373.6 96.9 reduce-scatter.28
  1472.7 9.0 reduce-scatter.24
  1484.0 183.3 reduce-scatter.26
  1669.7 11.9 reduce-scatter.20
  1685.9 138.2 all-reduce.13
where the time goes:
time: 1850 us; the launch traced here: 1840 us
  waiting for transfers between devices  1250 us (68%)
  matrix products  383 us (21%)
  other arithmetic  91.3 us (5%)
  local copies, waits for them, and re-layouts  61.5 us (3%)
  blocking collectives  39.4 us (2%)
    reduce_scatter x1, waiting for transfers between devices, body(): lax.psum_scatter(grad_w_qkv, 'row', scatter_dimension=2, tiled=True)  203 us
    reduce_scatter x1, waiting for transfers between devices, body(): lax.psum_scatter(grad_inner, 'row', scatter_dimension=2, tiled=True)  186 us
    reduce_scatter x1, waiting for transfers between devices, body(): lax.psum_scatter(value_terms, 'row', scatter_dimension=1, tiled=True)  143 us
    all_gather x1, waiting for transfers between devices, body(): lax.all_gather(qkv_cols, 'row', axis=2, tiled=True)  114 us
    psum x1, waiting for transfers between devices, body(): lax.psum((qkv_part, out_part, inner_part, mlp_part, gain_one, gain_two),...  102 us
    reduce_scatter x1, waiting for transfers between devices, body(): lax.psum_scatter(grad_w_mlp, 'row', scatter_dimension=1, tiled=True)  99.2 us
    all_gather x1, waiting for transfers between devices, body(): lax.all_gather(inner_cols, 'row', axis=2, tiled=True)  91.8 us
    dot_general x1, matrix products, attend_backward(): jnp.einsum('hqk,qhe->khe', grad_scores, query_heads, preferred_element_ty...  84.6 us
  transfers between devices with their start and end apart: 20, of which 19 were waited for; matrix products, arithmetic and copies ran while one was open for 18% of the time, Pallas kernels for 0%

commit v1 on v0

v1 whole, which is shorter than its diff:
```python
import jax
import jax.numpy as jnp
from jax import lax
from jax.experimental import pallas as pl
from jax.experimental.pallas import tpu as pltpu
from jax.sharding import PartitionSpec as P

HEADS = 16
HEAD = 64
EPSILON = 1e-05
ROPE_BASE = 160000.0
MASKED = -1e30
LOG2E = 1.4426950408889634
SCALE2 = HEAD ** (-0.5) * LOG2E
F32 = jnp.float32
BF16 = jnp.bfloat16
FQ, FK = 256, 512
BK, BQ = 256, 512


def layer_norm(inputs, gain):
    average = jnp.mean(inputs, axis=-1, keepdims=True)
    centred = inputs - average
    variance = jnp.mean(centred * centred, axis=-1, keepdims=True)
    return centred * lax.rsqrt(variance + EPSILON) * gain


def rotary(positions, heads):
    half_head = HEAD // 2
    frequency = jnp.power(ROPE_BASE, -2.0 * jnp.arange(half_head).astype(F32) / HEAD)
    angles = positions[:, None] * frequency[None, :]
    return (jnp.tile(jnp.cos(angles), (1, 2 * heads)), jnp.tile(jnp.sin(angles), (1, 2 * heads)))


def turned(flat):
    half = HEAD // 2
    ahead = jnp.concatenate([flat[:, half:], flat[:, :half]], axis=1)
    behind = jnp.concatenate([flat[:, -half:], flat[:, :-half]], axis=1)
    first = (lax.broadcasted_iota(jnp.int32, flat.shape, 1) % HEAD) < half
    return jnp.where(first, -ahead, behind)


def contract_rows(left_side, right_side):
    return lax.dot_general(
        left_side, right_side, (((0,), (0,)), ((), ())), preferred_element_type=F32
    )


def times_transpose(left_side, right_side):
    return lax.dot_general(
        left_side, right_side, (((1,), (1,)), ((), ())), preferred_element_type=F32
    )


def plain(left_side, right_side):
    return jnp.dot(left_side, right_side, preferred_element_type=F32)


def forward_kernel(bounds, q_ref, k_ref, vt_ref, segq_ref, segk_ref, o_ref, lse_ref, acc):
    block = pl.program_id(0)
    heads = lse_ref.shape[0]
    acc[...] = jnp.zeros_like(acc)
    seg_query = segq_ref[...]

    def step(tile, carry):
        rows = pl.ds(pl.multiple_of(tile * FK, FK), FK)
        allowed = segk_ref[rows, :] == seg_query
        kept = []
        for head in range(heads):
            highest, summed = carry[head]
            cols = slice(head * HEAD, (head + 1) * HEAD)
            logits = times_transpose(k_ref[rows, cols], q_ref[:, cols]) * SCALE2
            logits = jnp.where(allowed, logits, MASKED)
            higher = jnp.maximum(highest, jnp.max(logits, axis=0, keepdims=True))
            exponent = jnp.exp2(logits - higher)
            shrink = jnp.exp2(highest - higher)
            acc[cols, :] = acc[cols, :] * shrink + plain(
                vt_ref[cols, rows], exponent.astype(BF16)
            )
            kept.append((higher, summed * shrink + jnp.sum(exponent, axis=0, keepdims=True)))
        return tuple(kept)

    start = (jnp.full(seg_query.shape, MASKED, F32), jnp.zeros(seg_query.shape, F32))
    totals = lax.fori_loop(bounds[0, block], bounds[1, block], step, (start,) * heads)
    for head in range(heads):
        highest, summed = totals[head]
        cols = slice(head * HEAD, (head + 1) * HEAD)
        acc[cols, :] = acc[cols, :] / summed
        lse_ref[head : head + 1, :] = highest + jnp.log2(summed)
    o_ref[...] = acc[...].T.astype(BF16)


def backward_kernel(
    bounds, q_ref, do_ref, k_ref, kt_ref, v_ref, segk_ref, segq_ref, lse_ref, inner_ref,
    dq_ref, dk_ref, dv_ref, dqt, dk_acc, dv_acc,
):
    block = pl.program_id(0)
    heads = lse_ref.shape[0]

    @pl.when(block == 0)
    def _():
        dqt[...] = jnp.zeros_like(dqt)

    dk_acc[...] = jnp.zeros_like(dk_acc)
    dv_acc[...] = jnp.zeros_like(dv_acc)
    seg_key = segk_ref[...]

    def step(tile, carry):
        rows = pl.ds(pl.multiple_of(tile * BQ, BQ), BQ)
        allowed = seg_key == segq_ref[:, rows]
        for head in range(heads):
            cols = slice(head * HEAD, (head + 1) * HEAD)
            queries = q_ref[rows, cols]
            grads = do_ref[rows, cols]
            logits = times_transpose(k_ref[:, cols], queries) * SCALE2
            probs = jnp.exp2(logits - lse_ref[head : head + 1, rows])
            probs = jnp.where(allowed, probs, 0.0)
            grad_probs = times_transpose(v_ref[:, cols], grads)
            scores = (probs * (grad_probs - inner_ref[head : head + 1, rows])).astype(BF16)
            dv_acc[head] += plain(probs.astype(BF16), grads)
            dk_acc[head] += plain(scores, queries)
            dqt[cols, rows] += plain(kt_ref[cols, :], scores)
        return carry

    lax.fori_loop(bounds[0, block], bounds[1, block], step, 0)
    scale = HEAD ** (-0.5)
    for head in range(heads):
        cols = slice(head * HEAD, (head + 1) * HEAD)
        dk_ref[:, cols] = (dk_acc[head] * scale).astype(BF16)
        dv_ref[:, cols] = dv_acc[head].astype(BF16)

    @pl.when(block == pl.num_programs(0) - 1)
    def _():
        for tile in range(dq_ref.shape[0] // BQ):
            rows = slice(tile * BQ, (tile + 1) * BQ)
            dq_ref[rows, :] = (dqt[:, rows] * scale).T.astype(BF16)


def tile_bounds(seg, own, other):
    tiles = seg.reshape(-1, own)
    first = jnp.sum((seg[None, :] < tiles[:, :1]).astype(jnp.int32), axis=1)
    last = jnp.sum((seg[None, :] <= tiles[:, -1:]).astype(jnp.int32), axis=1)
    return jnp.stack([first // other, (last + other - 1) // other])


def attend(heads, qkv, seg):
    length, part = qkv.shape[0], heads * HEAD
    value_turned = qkv[:, 2 * part :].T
    return pl.pallas_call(
        forward_kernel,
        grid_spec=pltpu.PrefetchScalarGridSpec(
            num_scalar_prefetch=1,
            grid=(length // FQ,),
            in_specs=[
                pl.BlockSpec((FQ, part), lambda i, b: (i, 0)),
                pl.BlockSpec((length, part), lambda i, b: (0, 1)),
                pl.BlockSpec((part, length), lambda i, b: (0, 0)),
                pl.BlockSpec((1, FQ), lambda i, b: (0, i)),
                pl.BlockSpec((length, 1), lambda i, b: (0, 0)),
            ],
            out_specs=[
                pl.BlockSpec((FQ, part), lambda i, b: (i, 0)),
                pl.BlockSpec((heads, FQ), lambda i, b: (0, i)),
            ],
            scratch_shapes=[pltpu.VMEM((part, FQ), F32)],
        ),
        out_shape=[
            jax.ShapeDtypeStruct((length, part), BF16),
            jax.ShapeDtypeStruct((heads, length), F32),
        ],
        compiler_params=pltpu.CompilerParams(vmem_limit_bytes=40 * 2**20),
        cost_estimate=pl.CostEstimate(
            flops=4 * length * length * part, bytes_accessed=8 * length * part,
            transcendentals=length * length * heads,
        ),
        name="attend",
    )(tile_bounds(seg, FQ, FK), qkv, qkv, value_turned, seg[None, :], seg[:, None])


def attend_back(heads, qkv, seg, lse, inner, grads):
    length, part = qkv.shape[0], heads * HEAD
    key_turned = qkv[:, part : 2 * part].T
    return pl.pallas_call(
        backward_kernel,
        grid_spec=pltpu.PrefetchScalarGridSpec(
            num_scalar_prefetch=1,
            grid=(length // BK,),
            in_specs=[
                pl.BlockSpec((length, part), lambda i, b: (0, 0)),
                pl.BlockSpec((length, part), lambda i, b: (0, 0)),
                pl.BlockSpec((BK, part), lambda i, b: (i, 1)),
                pl.BlockSpec((part, BK), lambda i, b: (0, i)),
                pl.BlockSpec((BK, part), lambda i, b: (i, 2)),
                pl.BlockSpec((BK, 1), lambda i, b: (i, 0)),
                pl.BlockSpec((1, length), lambda i, b: (0, 0)),
                pl.BlockSpec((heads, length), lambda i, b: (0, 0)),
                pl.BlockSpec((heads, length), lambda i, b: (0, 0)),
            ],
            out_specs=[
                pl.BlockSpec((length, part), lambda i, b: (0, 0)),
                pl.BlockSpec((BK, part), lambda i, b: (i, 0)),
                pl.BlockSpec((BK, part), lambda i, b: (i, 0)),
            ],
            scratch_shapes=[
                pltpu.VMEM((part, length), F32),
                pltpu.VMEM((heads, BK, HEAD), F32),
                pltpu.VMEM((heads, BK, HEAD), F32),
            ],
        ),
        out_shape=[jax.ShapeDtypeStruct((length, part), BF16)] * 3,
        compiler_params=pltpu.CompilerParams(vmem_limit_bytes=48 * 2**20),
        cost_estimate=pl.CostEstimate(
            flops=10 * length * length * part, bytes_accessed=14 * length * part,
            transcendentals=length * length * heads,
        ),
        name="attend_back",
    )(
        tile_bounds(seg, BK, BQ), qkv, grads, qkv, key_turned, qkv,
        seg[:, None], seg[None, :], lse, inner,
    )


def gelu_parts(act):
    phi = 0.5 * (1.0 + lax.erf(act * 0.7071067811865476))
    bell = jnp.exp(act * act * -0.5) * 0.3989422804014327
    return act * phi, phi + act * bell


def body(tokens, segments, gain_attn, w_qkv, w_attn_out, gain_mlp, w_in, w_mlp, cotangent):
    _, local_rows, width = tokens.shape
    ranks = lax.axis_size("row")
    heads = HEADS // ranks
    part = heads * HEAD
    length = local_rows * ranks

    def gather(array, axis, dim):
        return lax.all_gather(array, axis, axis=dim, tiled=True)

    qkv_matrix = gather(gather(w_qkv, "row", 2), "col", 1).reshape(3 * width, width)
    seg = gather(segments, "row", 1).reshape(length)
    out_full = gather(gather(w_attn_out, "row", 1), "col", 0)
    inner_full = gather(w_in, "row", 2)
    mlp_full = gather(w_mlp, "row", 1)
    act_matrix, gate_matrix = inner_full[0], inner_full[1]
    hidden = inner_full.shape[1]

    def scatter_heads(parts):
        packed = jnp.stack([p.astype(BF16).reshape(local_rows, ranks, part) for p in parts], axis=2)
        packed = packed.transpose(1, 0, 2, 3).reshape(length, len(parts) * part)
        return lax.all_to_all(packed, "row", 0, 0, tiled=True)

    def gather_heads(packed):
        count = packed.shape[1] // part
        moved = lax.all_to_all(packed, "row", 0, 0, tiled=True)
        moved = moved.reshape(ranks, local_rows, count, part).transpose(2, 1, 0, 3)
        return moved.reshape(count, local_rows, width)

    inputs = tokens.astype(F32).reshape(local_rows, width)
    norm_one = layer_norm(inputs, gain_attn).astype(BF16)
    projected = times_transpose(norm_one, qkv_matrix)
    positions = (
        lax.axis_index("row") * local_rows + jnp.arange(local_rows, dtype=jnp.int32)
    ).astype(F32)
    cosine, sine = rotary(positions, HEADS)

    def rope(flat):
        return flat * cosine + turned(flat) * sine

    def rope_back(flat):
        return flat * cosine - turned(flat) * sine

    qkv = scatter_heads(
        [rope(projected[:, :width]), rope(projected[:, width : 2 * width]), projected[:, 2 * width :]]
    )
    attended, lse = attend(heads, qkv, seg)
    mixed = gather_heads(attended)[0]
    residual = inputs + times_transpose(mixed, out_full)
    norm_two = layer_norm(residual, gain_mlp).astype(BF16)
    mlp_inputs = gather(norm_two, "col", 0)
    mlp_cot = gather(cotangent.reshape(local_rows, width), "col", 0)

    act = times_transpose(mlp_inputs, act_matrix)
    gate = times_transpose(mlp_inputs, gate_matrix)
    grad_gated = times_transpose(mlp_cot, mlp_full)
    bent, slope = gelu_parts(act)
    gated = (bent * gate).astype(BF16)
    grad_act = (grad_gated * slope * gate).astype(BF16)
    grad_gate = (grad_gated * bent).astype(BF16)

    def over_col(array):
        return lax.psum_scatter(array.astype(BF16), "col", scatter_dimension=0, tiled=True)

    grad_norm_two = over_col(plain(grad_act, act_matrix) + plain(grad_gate, gate_matrix)).astype(F32)
    mlp_out = over_col(plain(gated, mlp_full)).astype(F32)
    output = (residual + mlp_out).astype(BF16).reshape(tokens.shape)

    second_back = jax.vjp(layer_norm, residual, gain_mlp)[1]
    grad_resid_part, grad_gain_mlp = second_back(grad_norm_two)
    grad_residual = cotangent.reshape(local_rows, width).astype(F32) + grad_resid_part
    grad_resid_low = grad_residual.astype(BF16)
    grad_mixed = scatter_heads([plain(grad_resid_low, out_full)])
    inner = jnp.sum(
        (grad_mixed.astype(F32) * attended.astype(F32)).reshape(length, heads, HEAD), axis=-1
    ).T
    back = attend_back(heads, qkv, seg, lse, inner, grad_mixed)

    def over_dp(array):
        return lax.psum_scatter(array.astype(BF16), "dp", scatter_dimension=0, tiled=True)

    def finish(array):
        owned = lax.psum_scatter(array, "row", scatter_dimension=1, tiled=True)
        return gather(owned, "dp", 0).astype(F32)

    grad_mlp_part = over_dp(contract_rows(gated, mlp_cot))
    grad_act_part = over_dp(contract_rows(grad_act, mlp_inputs))
    grad_gate_part = over_dp(contract_rows(grad_gate, mlp_inputs))
    grad_out_part = over_dp(over_col(contract_rows(grad_resid_low, mixed)))

    grad_raw = gather_heads(jnp.concatenate(back, axis=1)).astype(F32)
    grad_projected = jnp.concatenate(
        [rope_back(grad_raw[0]), rope_back(grad_raw[1]), grad_raw[2]], axis=1
    ).astype(BF16)
    grad_qkv = contract_rows(grad_projected, norm_one).astype(BF16)
    grad_qkv = lax.psum_scatter(
        grad_qkv.reshape(3, width, width), "col", scatter_dimension=1, tiled=True
    )
    grad_qkv_part = over_dp(grad_qkv.reshape(-1, width))
    grad_norm_one = plain(grad_projected, qkv_matrix)
    first_back = jax.vjp(layer_norm, inputs, gain_attn)[1]
    grad_in_part, grad_gain_attn = first_back(grad_norm_one)
    grad_input = (grad_residual + grad_in_part).astype(BF16).reshape(tokens.shape)

    grad_w_qkv = finish(grad_qkv_part).reshape(w_qkv.shape)
    grad_w_out = finish(grad_out_part)
    grad_w_in = jnp.stack([finish(grad_act_part), finish(grad_gate_part)])
    grad_w_mlp = finish(grad_mlp_part)
    gains = lax.psum(jnp.stack([grad_gain_attn, grad_gain_mlp]), ("dp", "row", "col"))
    size = width // (ranks * lax.axis_size("col"))
    place = (lax.axis_index("row") * lax.axis_size("col") + lax.axis_index("col")) * size
    gains = lax.dynamic_slice_in_dim(gains, place, size, axis=1)
    return (
        output, grad_input, grad_w_qkv, grad_w_out, grad_w_in, grad_w_mlp, gains[0], gains[1],
    )


def solution(mesh):
    return jax.shard_map(
        body,
        mesh=mesh,
        in_specs=(
            P(("dp", "col"), "row", None),
            P(("dp", "col"), "row"),
            P(),
            P(None, "col", "row"),
            P("col", "row"),
            P(),
            P(None, "col", "row"),
            P("col", "row"),
            P(("dp", "col"), "row", None),
        ),
        out_specs=(
            P(("dp", "col"), "row", None),
            P(("dp", "col"), "row", None),
            P(None, "col", "row"),
            P("col", "row"),
            P(None, "col", "row"),
            P("col", "row"),
            P(("row", "col")),
            P(("row", "col")),
        ),
        check_vma=False,
    )
```

time: 1850 us -> 998 us (0.54)
  waiting for transfers between devices: 1250 us -> 395 us
  matrix products: 383 us -> 95.3 us
  blocking collectives: 39.4 us -> 246 us
  Pallas kernels: 0 us -> 115 us
  other arithmetic: 91.3 us -> 33 us
    reduce_scatter x10 -> x11, waiting for transfers between devices: 739 us -> 111 us  [the longest x2 52.1 us: over_dp(): lax.psum_scatter(array.astype(BF16), 'dp', scatter_dimension=0, tiled=True)]
    dot_general x10 -> x5, matrix products: 318 us -> 30.8 us  [plain(): return jnp.dot(left_side, right_side, preferred_element_type=F32)]
    all_gather x9 -> x8, waiting for transfers between devices: 401 us -> 172 us  [gather(): return lax.all_gather(array, axis, axis=dim, tiled=True)]
    all_gather x2 -> x6, blocking collectives: 14.4 us -> 206 us  [gather(): return lax.all_gather(array, axis, axis=dim, tiled=True)]
    pallas_call x0 -> x2, Pallas kernels: none -> 115 us  [the longest x1 59.8 us: attend(): pl.pallas_call(forward_kernel, grid_spec=pltpu.PrefetchScalarGridSpec(num...]
    all_to_all x0 -> x4, waiting for transfers between devices: none -> 106 us  [the longest x2 87.8 us: gather_heads(): moved = lax.all_to_all(packed, 'row', 0, 0, tiled=True)]
    psum x1 -> x0, waiting for transfers between devices: 102 us -> none  [body(): lax.psum((qkv_part, out_part, inner_part, mlp_part, gain_one, gain_two),...]
    psum x1, blocking collectives: 10.6 us -> 39.7 us  [body(): lax.psum(jnp.stack([grad_gain_attn, grad_gain_mlp]), ('dp', 'row', 'col'))]
  transfers between devices with their start and end apart: 20 -> 26, of which waited for: 19 -> 15; matrix products, arithmetic and copies ran while one was open for 18% -> 16% of each run, Pallas kernels for 0% -> 12%
where the time goes in v1:
time: 998 us; the launch traced here: 987 us
  waiting for transfers between devices  395 us (40%)
  blocking collectives  246 us (25%)
  Pallas kernels  115 us (12%)
  matrix products  95.3 us (10%)
  local copies, waits for them, and re-layouts  67.9 us (7%)
  other arithmetic  33 us (3%)
  starting transfers between devices  19.9 us (2%)
  between operations  15.2 us (2%)
    all_gather x6, blocking collectives, gather(): return lax.all_gather(array, axis, axis=dim, tiled=True)  206 us
    all_gather x8, waiting for transfers between devices, gather(): return lax.all_gather(array, axis, axis=dim, tiled=True)  172 us
    all_to_all x2, waiting for transfers between devices, gather_heads(): moved = lax.all_to_all(packed, 'row', 0, 0, tiled=True)  87.8 us
    pallas_call x1, Pallas kernels, attend(): pl.pallas_call(forward_kernel, grid_spec=pltpu.PrefetchScalarGridSpec(num...  59.8 us
    pallas_call x1, Pallas kernels, attend_back(): pl.pallas_call(backward_kernel, grid_spec=pltpu.PrefetchScalarGridSpec(nu...  55.2 us
    reduce_scatter x2, waiting for transfers between devices, over_dp(): lax.psum_scatter(array.astype(BF16), 'dp', scatter_dimension=0, tiled=True)  52.1 us
    reduce_scatter x5, waiting for transfers between devices, finish(): owned = lax.psum_scatter(array, 'row', scatter_dimension=1, tiled=True)  47.8 us
    psum x1, blocking collectives, body(): lax.psum(jnp.stack([grad_gain_attn, grad_gain_mlp]), ('dp', 'row', 'col'))  39.7 us
  transfers between devices with their start and end apart: 26, of which 15 were waited for; matrix products, arithmetic and copies ran while one was open for 16% of the time, Pallas kernels for 12%

profile of v1, /device:TPU:0, one launch (start us, length us, event | category | flops | bytes accessed | tf_op | source)
XLA Modules:
  0.0 987.3 jit_solution(8494702097383500593)
XLA Ops:
  8.7 67.0 %all-gather.10.cloned.1.call-done = bf16[3,512,1024]{2,1,0:T(8,128)(2,1)} async-done(((bf16[3,512,256]{2,1,0:T(8,128)(2,1)}), bf16[3,512,1024]{2,1,0:T(8,128)(2,1)}) %all-gather.10.cloned.1.call-update) | async-done | bytes 3145744 | tf_op jit(solution)/shard_map/all_gather | solution.py:237
  77.7 1.9 copy.77
  79.7 1.7 tile.8
  81.4 3.0 copy.76
  85.1 20.6 %all-gather.14.cloned.1.call-done = bf16[512,1024]{1,0:T(8,128)(2,1)} async-done(((bf16[512,256]{1,0:T(8,128)(2,1)}), bf16[512,1024]{1,0:T(8,128)(2,1)}) %all-gather.14.cloned.1.call-update) | async-done | bytes 1048592 | tf_op jit(solution)/shard_map/all_gather | solution.py:237
  105.7 16.6 %all-gather.12.cloned.1.call-done = bf16[3,1024,1024]{2,1,0:T(8,128)(2,1)} async-done(((bf16[3,512,1024]{2,1,0:T(8,128)(2,1)}), bf16[3,1024,1024]{2,1,0:T(8,128)(2,1)}) %all-gather.12.cloned.1.call-update) | async-done | bytes 6291472 | tf_op jit(solution)/shard_map/all_gather | solution.py:237
  122.4 5.8 fusion.47
  128.2 2.7 copy-done.6
  134.0 5.4 fusion.67
  139.5 3.3 fusion.26
  145.7 3.2 pad_maximum_fusion
  148.9 5.0 all-to-all-start
  154.4 145.9 %all_gather.42.segq_ref = s32[1,2048]{1,0:T(1,128)S(1)} all-gather(s32[1,512]{1,0:T(1,128)S(1)} %copy-done.29), channel_id=1, replica_groups=mesh['dp'=4,'row'=4,'col'=2] {'row'}, dimensions={1}, use_global_device_ids=true | all-gather | bytes 10240 | tf_op jit(solution)/shard_map/all_gather | solution.py:237
  303.4 3.2 copy.83
  308.2 2.4 copy.84.vt_ref
  313.1 59.8 %attend.1 = (bf16[2048,256]{1,0:T(8,128)(2,1)S(1)}, f32[4,2048]{1,0:T(4,128)S(1)}) custom-call(s32[2,8]{1,0:T(2,128)S(1)} %pad_add_fusion.bounds, bf16[2048,768]{1,0:T(8,128)(2,1)S(1)} %bitcast.152, bf16[2048,768]{1,0:T(8,128)(2,1)S(1)} %bitcast.153, bf16[256,2048]{1,0:T(8,128)(2,1)S(1)} %copy-done.4, s32[1,2048]{1,0:T(1,128)S(1)} %all_gather.42.segq_ref, ...), custom_call_target="tpu_custom_call" | custom-call | flops 4294967296 | bytes 4194304 | tf_op jit(solution)/shard_map/attend/pallas_call | solution.py:149
  373.8 2.4 copy.86
  376.2 6.0 all-to-all-start.1
  382.2 22.0 %all-to-all-done.1 = bf16[4,512,256]{1,2,0:T(8,128)(2,1)S(1)} async-done(((bf16[4,512,256]{1,2,0:T(8,128)(2,1)}), bf16[4,512,256]{1,2,0:T(8,128)(2,1)S(1)}, u32[]{:S(2)}, u32[]{:S(2)}) %all-to-all-start.1) | async-done | bytes 1048608 | tf_op jit(solution)/shard_map/all_to_all | solution.py:254
  405.2 3.3 fusion.74
  412.3 8.7 all-gather.18.cloned.1.call-done
  421.0 7.9 fusion.13
  428.9 4.7 fusion.11
  434.3 58.7 %all-gather.22.cloned.1.call-done = bf16[1312,1024]{1,0:T(8,128)(2,1)} async-done(((bf16[1312,256]{1,0:T(8,128)(2,1)}), bf16[1312,1024]{1,0:T(8,128)(2,1)}) %all-gather.22.cloned.1.call-update) | async-done | bytes 2686992 | tf_op jit(solution)/shard_map/all_gather | solution.py:237
  493.0 11.1 %multiply_convert_fusion = (bf16[1024,1312]{0,1:T(8,128)(2,1)S(1)}, bf16[1024,1312]{0,1:T(8,128)(2,1)S(1)}, bf16[1024,1312]{0,1:T(8,128)(2,1)}) fusion(f32[1024,1312]{0,1:T(8,128)} %fusion.11, f32[1024,1312]{0,1:T(8,128)} %fusion.13, bf16[1312,1024]{1,0:T(8,128)(2,1)} %all-gather.22.cloned.1.call-done, bf16[1,1024,1024]{2,1,0:T(8,128)(2,1)} %all-gather.24.cloned.1.call-done), kind=kOutput, calls=%fused_computation.1 | convolution fusion | flops 2772959232 | bytes 23592960 | tf_op jit(solution)/shard_map/dot_general | solution.py:50
  504.1 7.3 fusion.10
  511.4 6.5 add_convert_fusion
  518.2 7.4 convolution_convert_fusion.5
  525.7 6.9 convolution_convert_fusion.1
  532.6 6.9 convolution_convert_fusion.2
  539.6 2.1 fusion.17
  541.7 3.5 fusion.65
  551.0 3.5 all-to-all-start.2
  555.6 7.1 convolution_convert_fusion.3
  562.7 17.9 %all-to-all-done.2 = bf16[4,512,256]{2,1,0:T(8,128)(2,1)S(1)} async-done(((bf16[4,512,256]{2,1,0:T(8,128)(2,1)}), bf16[4,512,256]{2,1,0:T(8,128)(2,1)S(1)}, u32[]{:S(2)}, u32[]{:S(2)}) %all-to-all-start.2) | async-done | bytes 1048608 | tf_op jit(solution)/shard_map/all_to_all | solution.py:250
  582.3 2.9 copy.88
  585.3 1.8 bitcast_reduce_fusion
  587.0 55.2 %attend_back.1 = (bf16[2048,256]{1,0:T(8,128)(2,1)S(1)}, bf16[2048,256]{1,0:T(8,128)(2,1)S(1)}, bf16[2048,256]{1,0:T(8,128)(2,1)S(1)}) custom-call(s32[2,8]{1,0:T(2,128)S(1)} %pad_add_fusion.bounds, bf16[2048,768]{1,0:T(8,128)(2,1)} %bitcast.154, bf16[2048,256]{1,0:T(8,128)(2,1)S(1)} %bitcast.158, bf16[2048,768]{1,0:T(8,128)(2,1)} %bitcast.155, ...), custom_call_target="tpu_custom_call" | custom-call | flops 10737418240 | bytes 7340032 | tf_op jit(solution)/shard_map/attend_back/pallas_call | solution.py:183
  642.5 2.9 copy.91
  645.4 3.7 all-to-all-start.3
  649.1 4.2 convolution_convert_fusion.4
  653.6 65.7 %all-to-all-done.3 = bf16[4,512,768]{1,2,0:T(8,128)(2,1)S(1)} async-done(((bf16[4,512,768]{1,2,0:T(8,128)(2,1)}), bf16[4,512,768]{1,2,0:T(8,128)(2,1)S(1)}, u32[]{:S(2)}, u32[]{:S(2)}) %all-to-all-start.3) | async-done | bytes 3145760 | tf_op jit(solution)/shard_map/all_to_all | solution.py:254
  720.3 2.3 copy.104
  722.6 2.7 fusion.68
  725.3 1.9 copy.102
  727.3 3.0 copy.103
  731.5 3.0 fusion.72
  737.4 2.5 fusion.34
  739.9 6.8 convolution_convert_fusion
  749.3 11.5 %reduce-scatter.25.cloned.1.call-done = bf16[3,512,1024]{2,1,0:T(8,128)(2,1)} async-done(((bf16[3,1024,1024]{2,1,0:T(8,128)(2,1)}), bf16[3,512,1024]{2,1,0:T(8,128)(2,1)}) %reduce-scatter.25.cloned.1.call-update) | async-done | bytes 3145744 | tf_op jit(solution)/shard_map/reduce_scatter | solution.py:324
  760.8 25.6 %reduce-scatter.41.cloned.1.call-done = bf16[328,256]{1,0:T(8,128)(2,1)} async-done(((bf16[328,1024]{1,0:T(8,128)(2,1)}), bf16[328,256]{1,0:T(8,128)(2,1)}) %reduce-scatter.41.cloned.1.call-update) | async-done | bytes 167952 | tf_op jit(solution)/shard_map/reduce_scatter | solution.py:311
  786.4 11.9 %all_gather.55 = bf16[1312,256]{1,0:T(8,128)(2,1)S(1)} all-gather(bf16[328,256]{1,0:T(8,128)(2,1)} %reduce-scatter.41.cloned.1.call-done), channel_id=1, replica_groups=mesh['dp'=4,'row'=4,'col'=2] {'dp'}, dimensions={0}, use_global_device_ids=true | all-gather | bytes 839680 | tf_op jit(solution)/shard_map/all_gather | solution.py:237
  799.5 10.5 %reduce-scatter.39.cloned.1.call-done = bf16[328,256]{1,0:T(8,128)(2,1)} async-done(((bf16[328,1024]{1,0:T(8,128)(2,1)}), bf16[328,256]{1,0:T(8,128)(2,1)}) %reduce-scatter.39.cloned.1.call-update) | async-done | bytes 167952 | tf_op jit(solution)/shard_map/reduce_scatter | solution.py:311
  810.0 11.9 %all_gather.54 = bf16[1312,256]{1,0:T(8,128)(2,1)S(1)} all-gather(bf16[328,256]{1,0:T(8,128)(2,1)} %reduce-scatter.39.cloned.1.call-done), channel_id=1, replica_groups=mesh['dp'=4,'row'=4,'col'=2] {'dp'}, dimensions={0}, use_global_device_ids=true | all-gather | bytes 839680 | tf_op jit(solution)/shard_map/all_gather | solution.py:237
  821.9 11.6 %reduce-scatter.37.cloned.1.call-done = bf16[328,256]{1,0:T(8,128)(2,1)} async-done(((bf16[328,1024]{1,0:T(8,128)(2,1)}), bf16[328,256]{1,0:T(8,128)(2,1)}) %reduce-scatter.37.cloned.1.call-update) | async-done | bytes 167952 | tf_op jit(solution)/shard_map/reduce_scatter | solution.py:311
  833.5 14.5 %all_gather.53 = bf16[1312,256]{1,0:T(8,128)(2,1)S(1)} all-gather(bf16[328,256]{1,0:T(8,128)(2,1)} %reduce-scatter.37.cloned.1.call-done), channel_id=1, replica_groups=mesh['dp'=4,'row'=4,'col'=2] {'dp'}, dimensions={0}, use_global_device_ids=true | all-gather | bytes 839680 | tf_op jit(solution)/shard_map/all_gather | solution.py:237
  849.7 13.6 %reduce-scatter.33.cloned.1.call-done = bf16[128,1024]{1,0:T(8,128)(2,1)} async-done(((bf16[512,1024]{1,0:T(8,128)(2,1)}), bf16[128,1024]{1,0:T(8,128)(2,1)}) %reduce-scatter.33.cloned.1.call-update) | async-done | bytes 262160 | tf_op jit(solution)/shard_map/reduce_scatter | solution.py:308
  863.4 8.3 fusion.19
  871.7 38.5 %reduce-scatter.27.cloned.1.call-done = bf16[384,1024]{1,0:T(8,128)(2,1)} async-done(((bf16[1536,1024]{1,0:T(8,128)(2,1)}), bf16[384,1024]{1,0:T(8,128)(2,1)}) %reduce-scatter.27.cloned.1.call-update) | async-done | bytes 786448 | tf_op jit(solution)/shard_map/reduce_scatter | solution.py:308
  910.2 2.6 fusion.15
  912.8 39.7 %psum.7 = f32[2,1024]{1,0:T(2,128)S(1)} all-reduce(f32[2,1024]{1,0:T(2,128)S(1)} %pad_maximum_fusion.5), channel_id=1, replica_groups=mesh['dp'=4,'row'=4,'col'=2] {'dp','row','col'}, use_global_device_ids=true, to_apply=%region_27.28 | all-reduce | flops 2048 | bytes 16384 | tf_op jit(solution)/shard_map/psum | solution.py:337
  953.0 3.2 fusion.45
  956.2 10.5 %all_gather.52 = bf16[512,256]{1,0:T(8,128)(2,1)S(1)} all-gather(bf16[128,256]{1,0:T(8,128)(2,1)} %reduce-scatter.35.cloned.1.call-done), channel_id=1, replica_groups=mesh['dp'=4,'row'=4,'col'=2] {'dp'}, dimensions={0}, use_global_device_ids=true | all-gather | bytes 327680 | tf_op jit(solution)/shard_map/all_gather | solution.py:237
  967.5 11.5 %all_gather.51 = bf16[1536,256]{1,0:T(8,128)(2,1)S(1)} all-gather(bf16[384,256]{1,0:T(8,128)(2,1)} %reduce-scatter.29.cloned.1.call-done), channel_id=1, replica_groups=mesh['dp'=4,'row'=4,'col'=2] {'dp'}, dimensions={0}, use_global_device_ids=true | all-gather | bytes 983040 | tf_op jit(solution)/shard_map/all_gather | solution.py:237
  (182 shorter events, 47.1 us)
Async XLA Ops:
  7.2 68.6 %all-gather.10.cloned.1.call-start = ((), (), s32[]{:S(2)}) async-start(), calls=%async_computation.18 | async-start | bytes 3932160 | tf_op jit(solution)/shard_map/all_gather | solution.py:237
  7.9 97.8 %all-gather.14.cloned.1.call-start = ((), (), s32[]{:S(2)}) async-start(), calls=%async_computation.20 | async-start | bytes 1310720 | tf_op jit(solution)/shard_map/all_gather | solution.py:237
  8.6 113.7 %all-gather.12.cloned.1.call-start = ((), (), s32[]{:S(2)}) async-start(), calls=%async_computation.19 | async-start | bytes 9437184 | tf_op jit(solution)/shard_map/all_gather | solution.py:237
  75.7 306.4 %all-gather.16.cloned.1.call-start = ((), (), s32[]{:S(2)}) async-start(), calls=%async_computation.21 | async-start | bytes 3145728 | tf_op jit(solution)/shard_map/all_gather | solution.py:237
  79.6 59.8 %copy-start.7 = (f32[512,1024]{1,0:T(8,128)}, f32[512,1024]{1,0:T(8,128)S(1)}, u32[]{:S(2)}) copy-start(f32[512,1024]{1,0:T(8,128)S(1)} %copy.77) | copy-start | bytes 6291460
  81.4 3.1 copy-start.13
  84.4 37.9 %copy-start.28 = (f32[1024]{0:T(1024)S(1)}, f32[1024]{0:T(1024)}, u32[]{:S(2)}) copy-start(f32[1024]{0:T(1024)} %param.11) | copy-start | bytes 12292
  85.1 43.0 %copy-start.26 = (f32[512]{0:T(512)}, f32[512]{0:T(512)S(1)}, u32[]{:S(2)}) copy-start(f32[512]{0:T(512)S(1)} %fusion.18) | copy-start | bytes 6148
  128.2 2.7 copy-start.6
  132.3 7.1 slice-start
  134.0 5.4 slice-start.1
  134.0 5.4 copy-start.9
  142.7 2.9 copy-start.18
  148.9 5.6 copy-start.29
  148.9 154.5 %all-to-all-start = ((bf16[4,512,768]{1,2,0:T(8,128)(2,1)}), bf16[4,512,768]{1,2,0:T(8,128)(2,1)}, u32[]{:S(2)}, u32[]{:S(2)}) async-start(bf16[4,512,768]{1,2,0:T(8,128)(2,1)} %bitcast.14), calls=%async_computation | async-start | bytes 6291456 | tf_op jit(solution)/shard_map/all_to_all | solution.py:250
  153.9 258.4 %all-gather.20.cloned.1.call-start = ((), (), s32[]{:S(2)}) async-start(), calls=%async_computation.23 | async-start | bytes 6717440 | tf_op jit(solution)/shard_map/all_gather | solution.py:237
  306.6 4.0 copy-start
  310.6 1.2 copy-start.3
  311.8 1.2 copy-start.4
  372.9 1.0 copy-start.1
  373.8 31.4 %copy-start.14 = (bf16[1,512,1024]{2,1,0:T(8,128)(2,1)S(1)}, bf16[1,512,1024]{2,1,0:T(8,128)(2,1)}, u32[]{:S(2)}) copy-start(bf16[1,512,1024]{2,1,0:T(8,128)(2,1)} %param.9) | copy-start | bytes 3145732
  376.2 28.0 %all-to-all-start.1 = ((bf16[4,512,256]{1,2,0:T(8,128)(2,1)}), bf16[4,512,256]{1,2,0:T(8,128)(2,1)S(1)}, u32[]{:S(2)}, u32[]{:S(2)}) async-start(bf16[4,512,256]{1,2,0:T(8,128)(2,1)} %copy.86), calls=%async_computation.1 | async-start | bytes 2097152 | tf_op jit(solution)/shard_map/all_to_all | solution.py:254
  382.2 38.8 %all-gather.18.cloned.1.call-start = ((), (), s32[]{:S(2)}) async-start(), calls=%async_computation.22 | async-start | bytes 3145728 | tf_op jit(solution)/shard_map/all_gather | solution.py:237
  404.2 1.0 copy-start.22
  408.5 0.7 copy-start.25
  410.5 23.7 %all-gather.24.cloned.1.call-start = ((), (), s32[]{:S(2)}) async-start(), calls=%async_computation.36 | async-start | bytes 3145728 | tf_op jit(solution)/shard_map/all_gather | solution.py:237
  411.3 81.7 %all-gather.22.cloned.1.call-start = ((), (), s32[]{:S(2)}) async-start(), calls=%async_computation.24 | async-start | bytes 3358720 | tf_op jit(solution)/shard_map/all_gather | solution.py:237
  412.0 127.5 %reduce-scatter.23.cloned.1.call-start = ((), (), s32[]{:S(2)}) async-start(), calls=%async_computation.26 | async-start | bytes 3145728 | tf_op jit(solution)/shard_map/reduce_scatter | solution.py:291
  421.0 7.9 copy-start.30
  421.0 7.9 copy-start.32
  504.1 7.3 copy-start.33
  504.1 7.3 copy-start.34
  517.9 23.8 %reduce-scatter.21.cloned.1.call-start = ((), (), s32[]{:S(2)}) async-start(), calls=%async_computation.25 | async-start | bytes 3145728 | tf_op jit(solution)/shard_map/reduce_scatter | solution.py:291
  525.6 221.1 %reduce-scatter.47.cloned.1.call-start = ((), (), s32[]{:S(2)}) async-start(), calls=%async_computation.39 | async-start | bytes 3358720
  532.6 214.8 %reduce-scatter.45.cloned.1.call-start = ((), (), s32[]{:S(2)}) async-start(), calls=%async_computation.38 | async-start | bytes 3358720
  541.7 3.5 copy-start.16
  545.2 1.3 copy-start.11
  545.2 2.6 copy-start.31
  546.5 1.0 copy-start.24
  549.9 5.1 copy-start.17
  551.0 29.6 %all-to-all-start.2 = ((bf16[4,512,256]{2,1,0:T(8,128)(2,1)}), bf16[4,512,256]{2,1,0:T(8,128)(2,1)S(1)}, u32[]{:S(2)}, u32[]{:S(2)}) async-start(bf16[4,512,256]{2,1,0:T(8,128)(2,1)} %bitcast.150), calls=%async_computation.4 | async-start | bytes 2097152 | tf_op jit(solution)/shard_map/all_to_all | solution.py:250
  554.5 193.4 %reduce-scatter.43.cloned.1.call-start = ((), (), s32[]{:S(2)}) async-start(), calls=%async_computation.37 | async-start | bytes 3358720
  562.7 17.9 %copy-start.2 = (bf16[2048,256]{1,0:T(8,128)(2,1)S(1)}, bf16[2048,256]{1,0:T(8,128)(2,1)}, u32[]{:S(2)}) copy-start(bf16[2048,256]{1,0:T(8,128)(2,1)} %copy-done.1) | copy-start | bytes 3145732
  645.4 73.9 %all-to-all-start.3 = ((bf16[4,512,768]{1,2,0:T(8,128)(2,1)}), bf16[4,512,768]{1,2,0:T(8,128)(2,1)S(1)}, u32[]{:S(2)}, u32[]{:S(2)}) async-start(bf16[4,512,768]{1,2,0:T(8,128)(2,1)} %copy.91), calls=%async_computation.5 | async-start | bytes 6291456 | tf_op jit(solution)/shard_map/all_to_all | solution.py:254
  649.1 99.5 %reduce-scatter.31.cloned.1.call-start = ((), (), s32[]{:S(2)}) async-start(), calls=%async_computation.30 | async-start | bytes 3145728 | tf_op jit(solution)/shard_map/reduce_scatter | solution.py:291
  653.3 107.4 %reduce-scatter.25.cloned.1.call-start = ((), (), s32[]{:S(2)}) async-start(), calls=%async_computation.27 | async-start | bytes 9437184 | tf_op jit(solution)/shard_map/reduce_scatter | solution.py:324
  734.5 1.6 copy-start.5
  734.5 2.2 copy-start.8
  734.5 2.8 copy-start.10
  737.4 2.5 copy-start.15
  737.4 2.5 copy-start.23
  739.9 6.8 copy-start.19
  739.9 6.8 copy-start.21
  746.7 39.7 %reduce-scatter.41.cloned.1.call-start = ((), (), s32[]{:S(2)}) async-start(), calls=%async_computation.35 | async-start | bytes 839680 | tf_op jit(solution)/shard_map/reduce_scatter | solution.py:311
  747.3 62.7 %reduce-scatter.39.cloned.1.call-start = ((), (), s32[]{:S(2)}) async-start(), calls=%async_computation.34 | async-start | bytes 839680 | tf_op jit(solution)/shard_map/reduce_scatter | solution.py:311
  747.9 85.6 %reduce-scatter.37.cloned.1.call-start = ((), (), s32[]{:S(2)}) async-start(), calls=%async_computation.33 | async-start | bytes 839680 | tf_op jit(solution)/shard_map/reduce_scatter | solution.py:311
  748.5 114.9 %reduce-scatter.33.cloned.1.call-start = ((), (), s32[]{:S(2)}) async-start(), calls=%async_computation.31 | async-start | bytes 1310720 | tf_op jit(solution)/shard_map/reduce_scatter | solution.py:308
  749.2 160.9 %reduce-scatter.27.cloned.1.call-start = ((), (), s32[]{:S(2)}) async-start(), calls=%async_computation.28 | async-start | bytes 3932160 | tf_op jit(solution)/shard_map/reduce_scatter | solution.py:308
  760.8 195.5 %reduce-scatter.35.cloned.1.call-start = ((), (), s32[]{:S(2)}) async-start(), calls=%async_computation.32 | async-start | bytes 327680 | tf_op jit(solution)/shard_map/reduce_scatter | solution.py:311
  848.0 15.4 %copy-start.20 = (bf16[512,1024]{1,0:T(8,128)(2,1)S(1)}, bf16[512,1024]{1,0:T(8,128)(2,1)}, u32[]{:S(2)}) copy-start(bf16[512,1024]{1,0:T(8,128)(2,1)} %copy-done.19) | copy-start | bytes 3145732
  863.3 46.8 %copy-start.27 = (f32[512]{0:T(512)S(1)}, f32[512]{0:T(512)}, u32[]{:S(2)}) copy-start(f32[512]{0:T(512)} %copy-done.26) | copy-start | bytes 6148
  863.4 104.2 %reduce-scatter.29.cloned.1.call-start = ((), (), s32[]{:S(2)}) async-start(), calls=%async_computation.29 | async-start | bytes 983040 | tf_op jit(solution)/shard_map/reduce_scatter | solution.py:311
  871.7 81.3 %copy-start.12 = (f32[512,1024]{1,0:T(8,128)S(1)}, f32[512,1024]{1,0:T(8,128)}, u32[]{:S(2)}) copy-start(f32[512,1024]{1,0:T(8,128)} %copy-done.11) | copy-start | bytes 6291460
Sparse Core Ops, SparseCore 0:
  9.6 66.1 all-gather.9
  77.3 28.3 all-gather.13
  107.2 15.0 all-gather.11
  123.7 11.7 all-gather.15
  155.9 155.8 all-gather.19
  410.7 10.2 all-gather.17
  422.5 11.7 all-gather.23
  435.8 57.0 all-gather.21
  518.0 7.7 reduce-scatter.22
  528.0 10.7 reduce-scatter.20
  541.9 41.3 reduce-scatter.46
  586.6 40.1 reduce-scatter.44
  629.8 40.1 reduce-scatter.42
  672.0 9.5 reduce-scatter.30
  746.8 13.8 reduce-scatter.24
  762.9 23.5 reduce-scatter.40
  788.7 21.3 reduce-scatter.38
  812.2 21.2 reduce-scatter.36
  836.7 26.6 reduce-scatter.32
  866.2 43.9 reduce-scatter.26
  912.4 19.6 reduce-scatter.34
  934.5 21.6 reduce-scatter.28

commit v2 on v1

--- a/solution.py
+++ b/solution.py
@@ -65,20 +65,30 @@
     def step(tile, carry):
         rows = pl.ds(pl.multiple_of(tile * FK, FK), FK)
         allowed = segk_ref[rows, :] == seg_query
-        kept = []
-        for head in range(heads):
-            highest, summed = carry[head]
-            cols = slice(head * HEAD, (head + 1) * HEAD)
-            logits = times_transpose(k_ref[rows, cols], q_ref[:, cols]) * SCALE2
-            logits = jnp.where(allowed, logits, MASKED)
-            higher = jnp.maximum(highest, jnp.max(logits, axis=0, keepdims=True))
-            exponent = jnp.exp2(logits - higher)
-            shrink = jnp.exp2(highest - higher)
-            acc[cols, :] = acc[cols, :] * shrink + plain(
-                vt_ref[cols, rows], exponent.astype(BF16)
+        spans = [slice(head * HEAD, (head + 1) * HEAD) for head in range(heads)]
+        logits = [
+            jnp.where(
+                allowed, times_transpose(k_ref[rows, cols], q_ref[:, cols]) * SCALE2, MASKED
             )
-            kept.append((higher, summed * shrink + jnp.sum(exponent, axis=0, keepdims=True)))
-        return tuple(kept)
+            for cols in spans
+        ]
+        higher = [
+            jnp.maximum(carry[head][0], jnp.max(logits[head], axis=0, keepdims=True))
+            for head in range(heads)
+        ]
+        exponents = [jnp.exp2(logits[head] - higher[head]) for head in range(heads)]
+        shrink = [jnp.exp2(carry[head][0] - higher[head]) for head in range(heads)]
+        sums = [
+            carry[head][1] * shrink[head] + jnp.sum(exponents[head], axis=0, keepdims=True)
+            for head in range(heads)
+        ]
+        terms = [
+            plain(vt_ref[cols, rows], exponents[head].astype(BF16))
+            for head, cols in enumerate(spans)
+        ]
+        for head, cols in enumerate(spans):
+            acc[cols, :] = acc[cols, :] * shrink[head] + terms[head]
+        return tuple(zip(higher, sums))
 
     start = (jnp.full(seg_query.shape, MASKED, F32), jnp.zeros(seg_query.shape, F32))
     totals = lax.fori_loop(bounds[0, block], bounds[1, block], step, (start,) * heads)
@@ -226,6 +236,63 @@
     return act * phi, phi + act * bell
 
 
+def swap(array, bit):
+    pairs = [(index, index ^ bit) for index in range(lax.axis_size("dp"))]
+    return lax.ppermute(array, "dp", pairs)
+
+
+def gather_first(piece):
+    half = piece.shape[1] // 2
+    left, right = piece[:, :half], piece[:, half:]
+    return jnp.stack([left, swap(left, 1)]), jnp.stack([right, swap(right, 2)])
+
+
+def gather_second(pairs):
+    left, right = pairs
+    return left, right, swap(left, 2), swap(right, 1)
+
+
+def gather_order(parts):
+    own = lax.axis_index("dp")
+    left, right, left_far, right_far = parts
+    near = jnp.concatenate(
+        [
+            jnp.concatenate([left, left_far]),
+            jnp.stack([right[0], right_far[0], right[1], right_far[1]]),
+        ],
+        axis=2,
+    )
+    return jnp.concatenate(
+        [lax.dynamic_slice_in_dim(near, index ^ own, 1) for index in range(4)]
+    )
+
+
+def gather_dp(piece):
+    return gather_order(gather_second(gather_first(piece)))
+
+
+def scatter_first(blocks):
+    half = blocks.shape[2] // 2
+    own = lax.axis_index("dp")
+    sides = []
+    for start, (first, second) in ((0, (1, 2)), (half, (2, 1))):
+        def block(index):
+            return lax.dynamic_slice(
+                blocks, (index ^ own, 0, start), (1, blocks.shape[1], half)
+            )
+        far = swap(jnp.concatenate([block(first), block(3)]), first)
+        near = block(0).astype(F32) + far[:1].astype(F32)
+        passed = (block(second).astype(F32) + far[1:].astype(F32)).astype(BF16)
+        sides.append((near, passed))
+    return sides
+
+
+def scatter_second(sides):
+    (near_a, passed_a), (near_b, passed_b) = sides
+    sums = [near_a + swap(passed_a, 2).astype(F32), near_b + swap(passed_b, 1).astype(F32)]
+    return jnp.concatenate([part.astype(BF16) for part in sums], axis=2)[0]
+
+
 def body(tokens, segments, gain_attn, w_qkv, w_attn_out, gain_mlp, w_in, w_mlp, cotangent):
     _, local_rows, width = tokens.shape
     ranks = lax.axis_size("row")
@@ -236,13 +303,28 @@
     def gather(array, axis, dim):
         return lax.all_gather(array, axis, axis=dim, tiled=True)
 
-    qkv_matrix = gather(gather(w_qkv, "row", 2), "col", 1).reshape(3 * width, width)
+    cols = lax.axis_size("col")
+    own_dp = lax.axis_index("dp")
+
+    def own_rows(array, dim):
+        size = array.shape[dim] // 4
+        return lax.dynamic_slice_in_dim(array, own_dp * size, size, axis=dim)
+
+    hidden = w_mlp.shape[0]
+    out_rows = w_attn_out.shape[0]
+    quarter, out_quarter = hidden // 4, out_rows // 4
     seg = gather(segments, "row", 1).reshape(length)
-    out_full = gather(gather(w_attn_out, "row", 1), "col", 0)
-    inner_full = gather(w_in, "row", 2)
-    mlp_full = gather(w_mlp, "row", 1)
-    act_matrix, gate_matrix = inner_full[0], inner_full[1]
-    hidden = inner_full.shape[1]
+    tokens, seg = lax.optimization_barrier((tokens, seg))
+    qkv_rows = gather(own_rows(w_qkv, 1).reshape(-1, w_qkv.shape[2]), "row", 1)
+    rest = jnp.concatenate(
+        [own_rows(w_in, 1).reshape(2 * quarter, -1), own_rows(w_mlp, 0), own_rows(w_attn_out, 0)]
+    )
+    rest, qkv_rows = lax.optimization_barrier((rest, qkv_rows))
+    qkv_near = gather_dp(qkv_rows).reshape(4, 3, out_quarter, width)
+    qkv_near = qkv_near.transpose(1, 0, 2, 3).reshape(3, out_rows, width)
+    qkv_matrix = gather(qkv_near, "col", 1).reshape(3 * width, width)
+    rest, qkv_late = lax.optimization_barrier((gather(rest, "row", 1), qkv_matrix))
+    rest_pairs = gather_first(rest)
 
     def scatter_heads(parts):
         packed = jnp.stack([p.astype(BF16).reshape(local_rows, ranks, part) for p in parts], axis=2)
@@ -272,7 +354,15 @@
     qkv = scatter_heads(
         [rope(projected[:, :width]), rope(projected[:, width : 2 * width]), projected[:, 2 * width :]]
     )
+    rest_pairs, qkv = lax.optimization_barrier((rest_pairs, qkv))
+    rest_parts = gather_second(rest_pairs)
     attended, lse = attend(heads, qkv, seg)
+    rest_parts, attended = lax.optimization_barrier((rest_parts, attended))
+    rest = gather_order(rest_parts)
+    act_matrix = rest[:, :quarter].reshape(hidden, width)
+    gate_matrix = rest[:, quarter : 2 * quarter].reshape(hidden, width)
+    mlp_full = rest[:, 2 * quarter : 3 * quarter].reshape(hidden, width)
+    out_full = gather(rest[:, 3 * quarter :].reshape(out_rows, width), "col", 0)
     mixed = gather_heads(attended)[0]
     residual = inputs + times_transpose(mixed, out_full)
     norm_two = layer_norm(residual, gain_mlp).astype(BF16)
@@ -302,42 +392,60 @@
     inner = jnp.sum(
         (grad_mixed.astype(F32) * attended.astype(F32)).reshape(length, heads, HEAD), axis=-1
     ).T
+    mlp_grads = [
+        contract_rows(grad_act, mlp_inputs),
+        contract_rows(grad_gate, mlp_inputs),
+        contract_rows(gated, mlp_cot),
+    ]
+    mlp_sides = scatter_first(
+        jnp.concatenate([g.astype(BF16).reshape(4, quarter, width) for g in mlp_grads], axis=1)
+    )
+    mlp_sides, grad_mixed = lax.optimization_barrier((mlp_sides, grad_mixed))
     back = attend_back(heads, qkv, seg, lse, inner, grad_mixed)
-
-    def over_dp(array):
-        return lax.psum_scatter(array.astype(BF16), "dp", scatter_dimension=0, tiled=True)
-
-    def finish(array):
-        owned = lax.psum_scatter(array, "row", scatter_dimension=1, tiled=True)
-        return gather(owned, "dp", 0).astype(F32)
-
-    grad_mlp_part = over_dp(contract_rows(gated, mlp_cot))
-    grad_act_part = over_dp(contract_rows(grad_act, mlp_inputs))
-    grad_gate_part = over_dp(contract_rows(grad_gate, mlp_inputs))
-    grad_out_part = over_dp(over_col(contract_rows(grad_resid_low, mixed)))
+    mlp_owned, back = lax.optimization_barrier((scatter_second(mlp_sides), back))
+
+    def finish(owned):
+        return gather_dp(lax.psum_scatter(owned, "row", scatter_dimension=1, tiled=True)).astype(F32)
 
     grad_raw = gather_heads(jnp.concatenate(back, axis=1)).astype(F32)
+    mlp_owned, grad_raw = lax.optimization_barrier((mlp_owned, grad_raw))
+    mlp_sums = finish(mlp_owned)
+    mlp_sums = [
+        mlp_sums[:, index * quarter : (index + 1) * quarter].reshape(hidden, -1) for index in range(3)
+    ]
+    grad_w_in, grad_w_mlp = jnp.stack(mlp_sums[:2]), mlp_sums[2]
+    grad_w_out = contract_rows(grad_resid_low, mixed).astype(BF16)
+
     grad_projected = jnp.concatenate(
         [rope_back(grad_raw[0]), rope_back(grad_raw[1]), grad_raw[2]], axis=1
     ).astype(BF16)
     grad_qkv = contract_rows(grad_projected, norm_one).astype(BF16)
-    grad_qkv = lax.psum_scatter(
-        grad_qkv.reshape(3, width, width), "col", scatter_dimension=1, tiled=True
-    )
-    grad_qkv_part = over_dp(grad_qkv.reshape(-1, width))
-    grad_norm_one = plain(grad_projected, qkv_matrix)
+    grad_norm_one = plain(grad_projected, qkv_late)
     first_back = jax.vjp(layer_norm, inputs, gain_attn)[1]
     grad_in_part, grad_gain_attn = first_back(grad_norm_one)
     grad_input = (grad_residual + grad_in_part).astype(BF16).reshape(tokens.shape)
 
-    grad_w_qkv = finish(grad_qkv_part).reshape(w_qkv.shape)
-    grad_w_out = finish(grad_out_part)
-    grad_w_in = jnp.stack([finish(grad_act_part), finish(grad_gate_part)])
-    grad_w_mlp = finish(grad_mlp_part)
-    gains = lax.psum(jnp.stack([grad_gain_attn, grad_gain_mlp]), ("dp", "row", "col"))
-    size = width // (ranks * lax.axis_size("col"))
-    place = (lax.axis_index("row") * lax.axis_size("col") + lax.axis_index("col")) * size
-    gains = lax.dynamic_slice_in_dim(gains, place, size, axis=1)
+    size = width // (ranks * cols)
+    gains = jnp.stack([grad_gain_attn, grad_gain_mlp]).astype(BF16)
+    gains = gains.reshape(2, ranks, cols, size).transpose(2, 1, 0, 3).reshape(cols, ranks, 2 * size)
+    gains = jnp.pad(gains, ((0, 0), (0, 0), (0, width // ranks - 2 * size)))
+    gains = jnp.pad(gains.reshape(cols, 1, 1, width), ((0, 0), (0, 3), (0, 15), (0, 0)))
+    packed = jnp.concatenate(
+        [
+            grad_qkv.reshape(3, cols, 4, out_quarter, width)
+            .transpose(1, 2, 0, 3, 4)
+            .reshape(cols, 4, 3 * out_quarter, width),
+            grad_w_out.reshape(cols, 4, out_quarter, width),
+            gains,
+        ],
+        axis=2,
+    )
+    packed = lax.psum_scatter(packed, "col", scatter_dimension=0, tiled=True)[0]
+    sums = finish(scatter_second(scatter_first(packed)))
+    grad_w_qkv = sums[:, : 3 * out_quarter].reshape(4, 3, out_quarter, -1)
+    grad_w_qkv = grad_w_qkv.transpose(1, 0, 2, 3).reshape(w_qkv.shape)
+    grad_w_out = sums[:, 3 * out_quarter : 4 * out_quarter].reshape(w_attn_out.shape)
+    gains = sums[0, 4 * out_quarter, : 2 * size].reshape(2, size)
     return (
         output, grad_input, grad_w_qkv, grad_w_out, grad_w_in, grad_w_mlp, gains[0], gains[1],
     )

time: 998 us -> 760 us (0.76)
  blocking collectives: 246 us -> 61.5 us
  waiting for transfers between devices: 395 us -> 273 us
  other arithmetic: 33 us -> 79.6 us
  local copies, waits for them, and re-layouts: 67.9 us -> 105 us
  starting transfers between devices: 19.9 us -> 50.1 us
  Pallas kernels: 115 us -> 87.8 us
  matrix products: 95.3 us -> 79 us
    all_gather x6 -> x2, blocking collectives: 206 us -> 33.7 us  [gather(): return lax.all_gather(array, axis, axis=dim, tiled=True)]
    ppermute x0 -> x24, waiting for transfers between devices: none -> 140 us  [swap(): return lax.ppermute(array, 'dp', pairs)]
    all_gather x8 -> x5, waiting for transfers between devices: 172 us -> 33.3 us  [gather(): return lax.all_gather(array, axis, axis=dim, tiled=True)]
    reduce_scatter x8 -> x3, waiting for transfers between devices: 111 us -> 18.8 us  [the longest x1 13.5 us: body(): packed = lax.psum_scatter(packed, 'col', scatter_dimension=0, tiled=True)[0]]
    psum x1 -> x0, blocking collectives: 39.7 us -> none  [body(): lax.psum(jnp.stack([grad_gain_attn, grad_gain_mlp]), ('dp', 'row', 'col'))]
    ppermute x0 -> x24, starting transfers between devices: none -> 34.6 us  [swap(): return lax.ppermute(array, 'dp', pairs)]
    all_to_all x0 -> x1, blocking collectives: none -> 27.8 us  [gather_heads(): moved = lax.all_to_all(packed, 'row', 0, 0, tiled=True)]
    pallas_call x1, Pallas kernels: 59.8 us -> 32.9 us  [attend(): pl.pallas_call(forward_kernel, grid_spec=pltpu.PrefetchScalarGridSpec(num...]
  transfers between devices with their start and end apart: 26 -> 37, of which waited for: 15 -> 24; matrix products, arithmetic and copies ran while one was open for 16% -> 18% of each run, Pallas kernels for 12% -> 12%
where the time goes in v2:
time: 760 us; the launch traced here: 752 us
  waiting for transfers between devices  273 us (36%)
  local copies, waits for them, and re-layouts  105 us (14%)
  Pallas kernels  87.8 us (12%)
  other arithmetic  79.6 us (10%)
  matrix products  79 us (10%)
  blocking collectives  61.5 us (8%)
  starting transfers between devices  50.1 us (7%)
  between operations  15.5 us (2%)
    ppermute x24, waiting for transfers between devices, swap(): return lax.ppermute(array, 'dp', pairs)  140 us
    all_to_all x1, waiting for transfers between devices, gather_heads(): moved = lax.all_to_all(packed, 'row', 0, 0, tiled=True)  65.6 us
    pallas_call x1, Pallas kernels, attend_back(): pl.pallas_call(backward_kernel, grid_spec=pltpu.PrefetchScalarGridSpec(nu...  54.9 us
    dot_general x5, matrix products, times_transpose(): lax.dot_general(left_side, right_side, (((1,), (1,)), ((), ())), preferre...  35.8 us
    ppermute x24, starting transfers between devices, swap(): return lax.ppermute(array, 'dp', pairs)  34.6 us
    all_gather x2, blocking collectives, gather(): return lax.all_gather(array, axis, axis=dim, tiled=True)  33.7 us
    all_gather x5, waiting for transfers between devices, gather(): return lax.all_gather(array, axis, axis=dim, tiled=True)  33.3 us
    pallas_call x1, Pallas kernels, attend(): pl.pallas_call(forward_kernel, grid_spec=pltpu.PrefetchScalarGridSpec(num...  32.9 us
  transfers between devices with their start and end apart: 37, of which 24 were waited for; matrix products, arithmetic and copies ran while one was open for 18% of the time, Pallas kernels for 12%

profile of v2, /device:TPU:0, one launch (start us, length us, event | category | flops | bytes accessed | tf_op | source)
XLA Modules:
  0.0 751.5 jit_solution(3261797951475088902)
XLA Ops:
  10.1 21.3 %all_gather.22 = bf16[384,1024]{1,0:T(8,128)(2,1)S(1)} all-gather(bf16[384,256]{1,0:T(8,128)(2,1)S(1)} %bitcast.284), channel_id=1, replica_groups=mesh['dp'=4,'row'=4,'col'=2] {'row'}, dimensions={1}, use_global_device_ids=true | all-gather | bytes 983040 | tf_op jit(solution)/shard_map/all_gather | solution.py:304
  35.5 5.2 collective-permute-done.2
  45.6 13.2 %collective-permute-done.3 = bf16[2,384,512]{2,1,0:T(8,128)(2,1)S(1)} collective-permute-done((bf16[2,384,512]{2,1,0:T(8,128)(2,1)}, bf16[2,384,512]{2,1,0:T(8,128)(2,1)S(1)}, u32[]{:S(2)}, u32[]{:S(2)}) %collective-permute-start.3) | collective-permute-done | bytes 786464 | tf_op jit(solution)/shard_map/ppermute | solution.py:241
  63.7 12.4 %all_gather.21 = s32[1,2048]{1,0:T(1,128)S(1)} all-gather(s32[1,512]{1,0:T(1,128)S(1)} %copy-done.49), channel_id=1, replica_groups=mesh['dp'=4,'row'=4,'col'=2] {'row'}, dimensions={1}, use_global_device_ids=true | all-gather | bytes 10240 | tf_op jit(solution)/shard_map/all_gather | solution.py:304
  83.0 2.9 copy.76
  86.0 8.3 %fusion.55 = f32[512,3072]{1,0:T(8,128)} fusion(bf16[3072,1024]{1,0:T(8,128)(2,1)} %bitcast.292, bf16[1,512,1024]{2,1,0:T(8,128)(2,1)S(1)} %copy-done.17, f32[1024]{0:T(1024)S(1)} %copy-done.45, f32[512]{0:T(512)S(1)} %fusion.68, f32[512]{0:T(512)S(1)} %broadcast_multiply_fusion.1), kind=kOutput, calls=%fused_computation.129 | convolution fusion | flops 3223846912 | bytes 13639680 | tf_op jit(solution)/shard_map/dot_general | solution.py:50
  96.1 8.7 %fusion.75 = (f32[512,992]{1,0:T(8,128)}, f32[512,992]{1,0:T(8,128)}, f32[512,992]{1,0:T(8,128)}, f32[512,992]{1,0:T(8,128)}) fusion(f32[512,3072]{1,0:T(8,128)} %fusion.55), kind=kLoop, calls=%fused_computation.226 | loop fusion | bytes 16252928 | tf_op jit(solution)/shard_map/slice | solution.py:38
  108.0 6.6 fusion.27
  117.5 3.2 pad_maximum_fusion.2
  120.7 4.6 all-to-all-start
  125.7 30.5 %all-gather.7.cloned.1.call-done = bf16[1112,1024]{1,0:T(8,128)(2,1)} async-done(((bf16[1112,256]{1,0:T(8,128)(2,1)}), bf16[1112,1024]{1,0:T(8,128)(2,1)}) %all-gather.7.cloned.1.call-update) | async-done | bytes 2277392 | tf_op jit(solution)/shard_map/all_gather | solution.py:304
  161.2 23.6 %collective-permute-done.5 = bf16[1112,512]{1,0:T(8,128)(2,1)S(1)} collective-permute-done((bf16[1112,512]{1,0:T(8,128)(2,1)S(1)}, bf16[1112,512]{1,0:T(8,128)(2,1)S(1)}, u32[]{:S(2)}, u32[]{:S(2)}) %collective-permute-start.5) | collective-permute-done | bytes 1138720 | tf_op jit(solution)/shard_map/ppermute | solution.py:241
  188.0 12.8 %all-to-all-done = bf16[4,512,768]{1,2,0:T(8,128)(2,1)} async-done(((bf16[4,512,768]{1,2,0:T(8,128)(2,1)}), bf16[4,512,768]{1,2,0:T(8,128)(2,1)}, u32[]{:S(2)}, u32[]{:S(2)}) %all-to-all-start) | async-done | bytes 3145760 | tf_op jit(solution)/shard_map/all_to_all | solution.py:332
  200.7 3.2 copy.83
  210.2 2.3 copy.84.vt_ref
  214.9 32.9 %attend.1 = (bf16[2048,256]{1,0:T(8,128)(2,1)S(1)}, f32[4,2048]{1,0:T(4,128)S(1)}) custom-call(s32[2,8]{1,0:T(2,128)S(1)} %pad_add_fusion.bounds, bf16[2048,768]{1,0:T(8,128)(2,1)S(1)} %bitcast.231, bf16[2048,768]{1,0:T(8,128)(2,1)S(1)} %bitcast.232, bf16[256,2048]{1,0:T(8,128)(2,1)S(1)} %copy-done.6, s32[1,2048]{1,0:T(1,128)S(1)} %all_gather.21, ...), custom_call_target="tpu_custom_call" | custom-call | flops 4294967296 | bytes 4194304 | tf_op jit(solution)/shard_map/attend/pallas_call | solution.py:159
  247.8 7.3 collective-permute-done.6
  259.1 3.9 maximum_maximum_fusion
  263.0 3.1 constant_dynamic-slice_fusion.15
  266.1 2.8 pad_maximum_fusion.19
  269.5 27.8 %all_to_all.42 = bf16[4,512,256]{1,2,0:T(8,128)(2,1)} all-to-all(bf16[4,512,256]{1,2,0:T(8,128)(2,1)S(1)} %copy.86), channel_id=1, replica_groups=mesh['dp'=4,'row'=4,'col'=2] {'row'}, dimensions={0} | all-to-all | bytes 2097152 | tf_op jit(solution)/shard_map/all_to_all | solution.py:336
  297.3 3.6 fusion.86
  304.0 5.9 pad_maximum_fusion.5
  312.2 7.8 %fusion.88 = f32[1024,1312]{0,1:T(8,128)} fusion(bf16[1024,1024]{1,0:T(8,128)(2,1)} %all-gather.13.cloned.1.call-done, bf16[1312,1024]{1,0:T(8,128)(2,1)} %bitcast.261), kind=kOutput, calls=%fused_computation.239 | convolution fusion | flops 2751463424 | bytes 10158080 | tf_op jit(solution)/shard_map/dot_general | solution.py:50
  320.0 4.7 fusion.87
  325.4 11.3 %fusion.4 = (bf16[1024,1312]{0,1:T(8,128)(2,1)S(1)}, bf16[1024,1312]{0,1:T(8,128)(2,1)S(1)}, bf16[1024,1312]{0,1:T(8,128)(2,1)}) fusion(f32[1024,1312]{0,1:T(8,128)} %fusion.87, f32[1024,1312]{0,1:T(8,128)} %fusion.88, bf16[1312,1024]{1,0:T(8,128)(2,1)} %bitcast.259, bf16[1,1024,1024]{2,1,0:T(8,128)(2,1)} %all-gather.15.cloned.1.call-done), kind=kOutput, calls=%fused_computation.11 | convolution fusion | flops 2772959232 | bytes 23592960 | tf_op jit(solution)/shard_map/dot_general | solution.py:50
  336.7 3.5 fusion.89
  340.4 4.7 add_convert_fusion
  345.4 7.4 convolution_convert_fusion.5
  352.8 5.6 convolution_convert_fusion.1
  358.5 3.2 convolution_convert_fusion.2
  361.7 3.2 convolution_convert_fusion.3
  374.6 3.4 fusion.73
  383.8 4.8 all-to-all-start.2
  390.1 24.2 %collective-permute-done.8 = bf16[2,984,512]{2,1,0:T(8,128)(2,1)} collective-permute-done((bf16[2,984,512]{2,1,0:T(8,128)(2,1)}, bf16[2,984,512]{2,1,0:T(8,128)(2,1)}, u32[]{:S(2)}, u32[]{:S(2)}) %collective-permute-start.8) | collective-permute-done | bytes 2015264 | tf_op jit(solution)/shard_map/ppermute | solution.py:241
  414.3 2.9 collective-permute-done.9
  417.2 6.4 add_convert_fusion.5
  425.2 2.9 copy.88
  432.6 54.9 %attend_back.1 = (bf16[2048,256]{1,0:T(8,128)(2,1)S(1)}, bf16[2048,256]{1,0:T(8,128)(2,1)S(1)}, bf16[2048,256]{1,0:T(8,128)(2,1)S(1)}) custom-call(s32[2,8]{1,0:T(2,128)S(1)} %pad_add_fusion.bounds, bf16[2048,768]{1,0:T(8,128)(2,1)} %bitcast.233, bf16[2048,256]{1,0:T(8,128)(2,1)S(1)} %bitcast.237, bf16[2048,768]{1,0:T(8,128)(2,1)} %bitcast.234, ...), custom_call_target="tpu_custom_call" | custom-call | flops 10737418240 | bytes 7340032 | tf_op jit(solution)/shard_map/attend_back/pallas_call | solution.py:193
  491.8 2.9 pad_maximum_fusion.3
  494.8 4.6 copy.91
  499.4 4.6 all-to-all-start.3
  504.0 4.2 convolution_convert_fusion.4
  508.2 65.6 %all-to-all-done.3 = bf16[4,512,768]{1,2,0:T(8,128)(2,1)S(1)} async-done(((bf16[4,512,768]{1,2,0:T(8,128)(2,1)}), bf16[4,512,768]{1,2,0:T(8,128)(2,1)S(1)}, u32[]{:S(2)}, u32[]{:S(2)}) %all-to-all-start.3) | async-done | bytes 3145760 | tf_op jit(solution)/shard_map/all_to_all | solution.py:336
  573.8 3.5 convert_bitcast_fusion
  577.3 8.0 %copy.92 = f32[3,512,4,256]{3,2,1,0:T(4,128)} copy(f32[3,512,4,256]{1,3,0,2:T(8,128)} %convert_bitcast_fusion) | data formatting | bytes 12582912 | tf_op jit(solution)/shard_map/convert_element_type | solution.py:410
  585.4 8.3 %reshape.478 = f32[3,512,1024]{2,1,0:T(8,128)} reshape(f32[3,512,4,256]{3,2,1,0:T(4,128)} %copy.92) | data formatting | bytes 12582912 | tf_op jit(solution)/shard_map/convert_element_type | solution.py:410
  595.4 2.5 slice_bitcast_fusion.1
  602.4 2.5 fusion.35
  605.0 6.7 convolution_convert_fusion
  611.6 3.6 fusion.20
  617.6 3.6 copy.97
  621.3 4.1 fusion.1
  626.4 13.5 %reduce-scatter.10.cloned.1.call-done = bf16[1,4,528,1024]{3,2,1,0:T(8,128)(2,1)} async-done(((bf16[2,4,528,1024]{3,2,1,0:T(8,128)(2,1)}), bf16[1,4,528,1024]{3,2,1,0:T(8,128)(2,1)}) %reduce-scatter.10.cloned.1.call-update) | async-done | bytes 4325392 | tf_op jit(solution)/shard_map/reduce_scatter | solution.py:443
  645.1 22.6 %collective-permute-done.12 = bf16[2,528,512]{2,1,0:T(8,128)(2,1)S(1)} collective-permute-done((bf16[2,528,512]{2,1,0:T(8,128)(2,1)S(1)}, bf16[2,528,512]{2,1,0:T(8,128)(2,1)S(1)}, u32[]{:S(2)}, u32[]{:S(2)}) %collective-permute-start.12) | collective-permute-done | bytes 1081376 | tf_op jit(solution)/shard_map/ppermute | solution.py:241
  669.8 12.0 %collective-permute-done.13 = bf16[1,528,512]{2,1,0:T(8,128)(2,1)S(1)} collective-permute-done((bf16[1,528,512]{2,1,0:T(8,128)(2,1)S(1)}, bf16[1,528,512]{2,1,0:T(8,128)(2,1)S(1)}, u32[]{:S(2)}, u32[]{:S(2)}) %collective-permute-start.13) | collective-permute-done | bytes 540704 | tf_op jit(solution)/shard_map/ppermute | solution.py:241
  684.0 11.3 %collective-permute-done.15 = bf16[1,528,512]{2,1,0:T(8,128)(2,1)S(1)} collective-permute-done((bf16[1,528,512]{2,1,0:T(8,128)(2,1)S(1)}, bf16[1,528,512]{2,1,0:T(8,128)(2,1)S(1)}, u32[]{:S(2)}, u32[]{:S(2)}) %collective-permute-start.15) | collective-permute-done | bytes 540704 | tf_op jit(solution)/shard_map/ppermute | solution.py:241
  701.3 3.1 collective-permute-done.22
  708.5 3.1 fusion.52
  711.6 5.2 collective-permute-done.23
  717.9 2.3 maximum_convert_fusion
  720.2 5.3 reduce-scatter.12.cloned.1.call-done
  729.6 3.6 fusion.76
  736.6 4.2 collective-permute-done.19
  (288 shorter events, 127.9 us)
Async XLA Ops:
  7.2 78.8 %all-gather.9.cloned.1.call-start = ((), (), s32[]{:S(2)}) async-start(), calls=%async_computation.10 | async-start | bytes 9437184 | tf_op jit(solution)/shard_map/all_gather | solution.py:304
  32.4 8.3 %collective-permute-start.2 = (bf16[384,512]{1,0:T(8,128)(2,1)S(1)}, bf16[384,512]{1,0:T(8,128)(2,1)S(1)}, u32[]{:S(2)}, u32[]{:S(2)}) collective-permute-start(bf16[384,512]{1,0:T(8,128)(2,1)S(1)} %get-tuple-element.156), channel_id=1, source_target_pairs={{0,16},{8,24},{16,0},{24,8},{1,17},{9,25},{17,1},{25,9},{2,18},{10... | collective-permute-start | bytes 1179656 | tf_op jit(solution)/shard_map/ppermute | solution.py:241
  34.0 9.1 %collective-permute-start = (bf16[384,512]{1,0:T(8,128)(2,1)S(1)}, bf16[384,512]{1,0:T(8,128)(2,1)S(1)}, u32[]{:S(2)}, u32[]{:S(2)}) collective-permute-start(bf16[384,512]{1,0:T(8,128)(2,1)S(1)} %get-tuple-element.157), channel_id=1, source_target_pairs={{0,8},{8,0},{16,24},{24,16},{1,9},{9,1},{17,25},{25,17},{2,10},{10... | collective-permute-start | bytes 1179656 | tf_op jit(solution)/shard_map/ppermute | solution.py:241
  41.6 17.1 %collective-permute-start.3 = (bf16[2,384,512]{2,1,0:T(8,128)(2,1)}, bf16[2,384,512]{2,1,0:T(8,128)(2,1)S(1)}, u32[]{:S(2)}, u32[]{:S(2)}) collective-permute-start(bf16[2,384,512]{2,1,0:T(8,128)(2,1)} %pad_maximum_fusion.21), channel_id=1, source_target_pairs={{0,8},{8,0},{16,24},{24,16},{1,9},{9,1},{17,25},{25,17},{2,10},{10... | collective-permute-start | bytes 2359304 | tf_op jit(solution)/shard_map/ppermute | solution.py:241
  44.1 15.6 %collective-permute-start.1 = (bf16[2,384,512]{2,1,0:T(8,128)(2,1)}, bf16[2,384,512]{2,1,0:T(8,128)(2,1)S(1)}, u32[]{:S(2)}, u32[]{:S(2)}) collective-permute-start(bf16[2,384,512]{2,1,0:T(8,128)(2,1)} %pad_maximum_fusion.20), channel_id=1, source_target_pairs={{0,16},{8,24},{16,0},{24,8},{1,17},{9,25},{17,1},{25,9},{2,18},{10... | collective-permute-start | bytes 2359304 | tf_op jit(solution)/shard_map/ppermute | solution.py:241
  62.9 13.3 %copy-start.17 = (bf16[1,512,1024]{2,1,0:T(8,128)(2,1)S(1)}, bf16[1,512,1024]{2,1,0:T(8,128)(2,1)}, u32[]{:S(2)}) copy-start(bf16[1,512,1024]{2,1,0:T(8,128)(2,1)} %param.9) | copy-start | bytes 3145732
  62.9 93.3 %all-gather.7.cloned.1.call-start = ((), (), s32[]{:S(2)}) async-start(), calls=%async_computation.9 | async-start | bytes 2846720 | tf_op jit(solution)/shard_map/all_gather | solution.py:304
  63.7 44.0 %copy-start.47 = (pred[1024]{0:T(1024)(128)(4,1)}, pred[1024]{0:T(1024)(128)(4,1)S(1)}, u32[]{:S(2)}) copy-start(pred[1024]{0:T(1024)(128)(4,1)S(1)} %fusion.67) | copy-start | bytes 3076
  63.7 43.9 %copy-start.35 = (s32[1024]{0:T(1024)}, s32[1024]{0:T(1024)S(1)}, u32[]{:S(2)}) copy-start(s32[1024]{0:T(1024)S(1)} %get-tuple-element.180) | copy-start | bytes 12292
  63.7 43.9 %copy-start.37 = (s32[1024]{0:T(1024)}, s32[1024]{0:T(1024)S(1)}, u32[]{:S(2)}) copy-start(s32[1024]{0:T(1024)S(1)} %get-tuple-element.181) | copy-start | bytes 12292
  76.4 9.6 %copy-start.39 = (f32[512]{0:T(512)}, f32[512]{0:T(512)S(1)}, u32[]{:S(2)}) copy-start(f32[512]{0:T(512)S(1)} %broadcast_multiply_fusion.1) | copy-start | bytes 6148
  77.4 8.6 %copy-start.43 = (f32[512]{0:T(512)}, f32[512]{0:T(512)S(1)}, u32[]{:S(2)}) copy-start(f32[512]{0:T(512)S(1)} %fusion.68) | copy-start | bytes 6148
  81.2 26.4 %copy-start.11 = (f32[512,1024]{1,0:T(8,128)}, f32[512,1024]{1,0:T(8,128)S(1)}, u32[]{:S(2)}) copy-start(f32[512,1024]{1,0:T(8,128)S(1)} %copy.77) | copy-start | bytes 6291460
  120.7 80.0 %all-to-all-start = ((bf16[4,512,768]{1,2,0:T(8,128)(2,1)}), bf16[4,512,768]{1,2,0:T(8,128)(2,1)}, u32[]{:S(2)}, u32[]{:S(2)}) async-start(bf16[4,512,768]{1,2,0:T(8,128)(2,1)} %bitcast.23), calls=%async_computation | async-start | bytes 6291456 | tf_op jit(solution)/shard_map/all_to_all | solution.py:332
  125.4 171.9 %all-gather.11.cloned.1.call-start = ((), (), s32[]{:S(2)}) async-start(), calls=%async_computation.11 | async-start | bytes 3145728 | tf_op jit(solution)/shard_map/all_gather | solution.py:304
  158.2 26.6 %collective-permute-start.5 = (bf16[1112,512]{1,0:T(8,128)(2,1)S(1)}, bf16[1112,512]{1,0:T(8,128)(2,1)S(1)}, u32[]{:S(2)}, u32[]{:S(2)}) collective-permute-start(bf16[1112,512]{1,0:T(8,128)(2,1)S(1)} %get-tuple-element.133), channel_id=1, source_target_pairs={{0,16},{8,24},{16,0},{24,8},{1,17},{9,25},{17,1},{25,9},{2,18},{10... | collective-permute-start | bytes 3416072 | tf_op jit(solution)/shard_map/ppermute | solution.py:241
  159.5 26.9 %collective-permute-start.4 = (bf16[1112,512]{1,0:T(8,128)(2,1)S(1)}, bf16[1112,512]{1,0:T(8,128)(2,1)S(1)}, u32[]{:S(2)}, u32[]{:S(2)}) collective-permute-start(bf16[1112,512]{1,0:T(8,128)(2,1)S(1)} %get-tuple-element.134), channel_id=1, source_target_pairs={{0,8},{8,0},{16,24},{24,16},{1,9},{9,1},{17,25},{25,17},{2,10},{10... | collective-permute-start | bytes 3416072 | tf_op jit(solution)/shard_map/ppermute | solution.py:241
  203.9 8.5 %copy-start.2 = (bf16[4,512,768]{2,1,0:T(8,128)(2,1)}, bf16[4,512,768]{2,1,0:T(8,128)(2,1)S(1)}, u32[]{:S(2)}) copy-start(bf16[4,512,768]{2,1,0:T(8,128)(2,1)S(1)} %copy.83) | copy-start | bytes 9437188
  203.9 51.2 %collective-permute-start.6 = (bf16[2,1112,512]{2,1,0:T(8,128)(2,1)}, bf16[2,1112,512]{2,1,0:T(8,128)(2,1)}, u32[]{:S(2)}, u32[]{:S(2)}) collective-permute-start(bf16[2,1112,512]{2,1,0:T(8,128)(2,1)} %pad_maximum_fusion.11), channel_id=1, source_target_pairs={{0,16},{8,24},{16,0},{24,8},{1,17},{9,25},{17,1},{25,9},{2,18},{10... | collective-permute-start | bytes 6832136 | tf_op jit(solution)/shard_map/ppermute | solution.py:241
  205.5 51.1 %collective-permute-start.7 = (bf16[2,1112,512]{2,1,0:T(8,128)(2,1)}, bf16[2,1112,512]{2,1,0:T(8,128)(2,1)}, u32[]{:S(2)}, u32[]{:S(2)}) collective-permute-start(bf16[2,1112,512]{2,1,0:T(8,128)(2,1)} %pad_maximum_fusion.12), channel_id=1, source_target_pairs={{0,8},{8,0},{16,24},{24,16},{1,9},{9,1},{17,25},{25,17},{2,10},{10... | collective-permute-start | bytes 6832136 | tf_op jit(solution)/shard_map/ppermute | solution.py:241
  214.9 41.7 %copy-start.21 = (bf16[2,1112,512]{2,1,0:T(8,128)(2,1)S(1)}, bf16[2,1112,512]{2,1,0:T(8,128)(2,1)}, u32[]{:S(2)}) copy-start(bf16[2,1112,512]{2,1,0:T(8,128)(2,1)} %pad_maximum_fusion.12) | copy-start | bytes 6832132
  247.8 8.9 %copy-start.3 = (bf16[2048,256]{1,0:T(8,128)(2,1)}, bf16[2048,256]{1,0:T(8,128)(2,1)S(1)}, u32[]{:S(2)}) copy-start(bf16[2048,256]{1,0:T(8,128)(2,1)S(1)} %get-tuple-element.47) | copy-start | bytes 3145732
  268.9 43.3 %all-gather.13.cloned.1.call-start = ((), (), s32[]{:S(2)}) async-start(), calls=%async_computation.12 | async-start | bytes 3145728 | tf_op jit(solution)/shard_map/all_gather | solution.py:304
  302.9 22.5 %all-gather.15.cloned.1.call-start = ((), (), s32[]{:S(2)}) async-start(), calls=%async_computation.18 | async-start | bytes 3145728 | tf_op jit(solution)/shard_map/all_gather | solution.py:304
  303.5 69.0 %reduce-scatter.8.cloned.1.call-start = ((), (), s32[]{:S(2)}) async-start(), calls=%async_computation.14 | async-start | bytes 3145728 | tf_op jit(solution)/shard_map/reduce_scatter | solution.py:381
  312.2 7.8 %copy-start.29 = (bf16[4,328,1024]{2,1,0:T(8,128)(2,1)S(1)}, bf16[4,328,1024]{2,1,0:T(8,128)(2,1)}, u32[]{:S(2)}) copy-start(bf16[4,328,1024]{2,1,0:T(8,128)(2,1)} %get-tuple-element.91) | copy-start | bytes 8060932
  312.2 7.8 %copy-start.51 = (bf16[1024,1024]{1,0:T(8,128)(2,1)S(1)}, bf16[1024,1024]{1,0:T(8,128)(2,1)}, u32[]{:S(2)}) copy-start(bf16[1024,1024]{1,0:T(8,128)(2,1)} %all-gather.13.cloned.1.call-done) | copy-start | bytes 6291460
  325.4 11.3 %copy-start.30 = (bf16[4,328,1024]{2,1,0:T(8,128)(2,1)S(1)}, bf16[4,328,1024]{2,1,0:T(8,128)(2,1)}, u32[]{:S(2)}) copy-start(bf16[4,328,1024]{2,1,0:T(8,128)(2,1)} %get-tuple-element.91) | copy-start | bytes 8060932
  336.7 3.5 copy-start.53
  336.7 3.5 copy-start.55
  336.7 3.7 copy-start.28
  345.1 29.5 %reduce-scatter.6.cloned.1.call-start = ((), (), s32[]{:S(2)}) async-start(), calls=%async_computation.13 | async-start | bytes 3145728 | tf_op jit(solution)/shard_map/reduce_scatter | solution.py:381
  352.8 5.7 copy-start.52
  352.8 5.7 copy-start.56
  365.6 5.5 copy-start.9
  367.9 46.4 %collective-permute-start.8 = (bf16[2,984,512]{2,1,0:T(8,128)(2,1)}, bf16[2,984,512]{2,1,0:T(8,128)(2,1)}, u32[]{:S(2)}, u32[]{:S(2)}) collective-permute-start(bf16[2,984,512]{2,1,0:T(8,128)(2,1)} %pad_maximum_fusion.13), channel_id=1, source_target_pairs={{0,8},{8,0},{16,24},{24,16},{1,9},{9,1},{17,25},{25,17},{2,10},{10... | collective-permute-start | bytes 6045704 | tf_op jit(solution)/shard_map/ppermute | solution.py:241
  371.0 46.1 %collective-permute-start.9 = (bf16[2,984,512]{2,1,0:T(8,128)(2,1)}, bf16[2,984,512]{2,1,0:T(8,128)(2,1)}, u32[]{:S(2)}, u32[]{:S(2)}) collective-permute-start(bf16[2,984,512]{2,1,0:T(8,128)(2,1)} %pad_maximum_fusion.14), channel_id=1, source_target_pairs={{0,16},{8,24},{16,0},{24,8},{1,17},{9,25},{17,1},{25,9},{2,18},{10... | collective-permute-start | bytes 6045704 | tf_op jit(solution)/shard_map/ppermute | solution.py:241
  383.8 39.9 %all-to-all-start.2 = ((bf16[4,512,256]{2,1,0:T(8,128)(2,1)}), bf16[4,512,256]{2,1,0:T(8,128)(2,1)S(1)}, u32[]{:S(2)}, u32[]{:S(2)}) async-start(bf16[4,512,256]{2,1,0:T(8,128)(2,1)} %bitcast.229), calls=%async_computation.4 | async-start | bytes 2097152 | tf_op jit(solution)/shard_map/all_to_all | solution.py:332
  428.1 59.4 %collective-permute-start.10 = (bf16[1,984,512]{2,1,0:T(8,128)(2,1)}, bf16[1,984,512]{2,1,0:T(8,128)(2,1)S(1)}, u32[]{:S(2)}, u32[]{:S(2)}) collective-permute-start(bf16[1,984,512]{2,1,0:T(8,128)(2,1)} %get-tuple-element.53), channel_id=1, source_target_pairs={{0,16},{8,24},{16,0},{24,8},{1,17},{9,25},{17,1},{25,9},{2,18},{10... | collective-permute-start | bytes 3022856 | tf_op jit(solution)/shard_map/ppermute | solution.py:241
  431.4 56.5 %collective-permute-start.11 = (bf16[1,984,512]{2,1,0:T(8,128)(2,1)S(1)}, bf16[1,984,512]{2,1,0:T(8,128)(2,1)S(1)}, u32[]{:S(2)}, u32[]{:S(2)}) collective-permute-start(bf16[1,984,512]{2,1,0:T(8,128)(2,1)S(1)} %copy-done.33), channel_id=1, source_target_pairs={{0,8},{8,0},{16,24},{24,16},{1,9},{9,1},{17,25},{25,17},{2,10},{10... | collective-permute-start | bytes 3022856 | tf_op jit(solution)/shard_map/ppermute | solution.py:241
  432.6 55.0 %copy-start.25 = (f32[1,984,512]{2,1,0:T(8,128)S(1)}, f32[1,984,512]{2,1,0:T(8,128)}, u32[]{:S(2)}) copy-start(f32[1,984,512]{2,1,0:T(8,128)} %get-tuple-element.52) | copy-start | bytes 6045700
  499.4 74.4 %all-to-all-start.3 = ((bf16[4,512,768]{1,2,0:T(8,128)(2,1)}), bf16[4,512,768]{1,2,0:T(8,128)(2,1)S(1)}, u32[]{:S(2)}, u32[]{:S(2)}) async-start(bf16[4,512,768]{1,2,0:T(8,128)(2,1)} %copy.91), calls=%async_computation.5 | async-start | bytes 6291456 | tf_op jit(solution)/shard_map/all_to_all | solution.py:336
  504.0 135.9 %reduce-scatter.10.cloned.1.call-start = ((), (), s32[]{:S(2)}) async-start(), calls=%async_computation.15 | async-start | bytes 12976128 | tf_op jit(solution)/shard_map/reduce_scatter | solution.py:443
  602.4 9.2 %slice-start.2 = ((s8[6291456]{0:T(1024)(128)(4,1)}), s8[2097152]{0:T(1024)(128)(4,1)S(1)}, s32[]{:S(2)}) async-start(s8[6291456]{0:T(1024)(128)(4,1)} %bitcast.293), calls=%async_computation.21 | async-start | bytes 4194304
  604.9 6.7 slice-start.3
  611.6 3.6 copy-start.42
  617.6 3.7 copy-start.31
  625.4 71.3 %reduce-scatter.14.cloned.1.call-start = ((), (), s32[]{:S(2)}) async-start(), calls=%async_computation.17 | async-start | bytes 2519040 | tf_op jit(solution)/shard_map/reduce_scatter | solution.py:408
  626.1 99.4 %reduce-scatter.12.cloned.1.call-start = ((), (), s32[]{:S(2)}) async-start(), calls=%async_computation.16 | async-start | bytes 1351680 | tf_op jit(solution)/shard_map/reduce_scatter | solution.py:408
  641.5 26.2 %copy-start.26 = (bf16[1,4,528,1024]{3,2,1,0:T(8,128)(2,1)S(1)}, bf16[1,4,528,1024]{3,2,1,0:T(8,128)(2,1)}, u32[]{:S(2)}) copy-start(bf16[1,4,528,1024]{3,2,1,0:T(8,128)(2,1)} %reduce-scatter.10.cloned.1.call-done) | copy-start | bytes 12976132
  641.7 26.1 %collective-permute-start.12 = (bf16[2,528,512]{2,1,0:T(8,128)(2,1)S(1)}, bf16[2,528,512]{2,1,0:T(8,128)(2,1)S(1)}, u32[]{:S(2)}, u32[]{:S(2)}) collective-permute-start(bf16[2,528,512]{2,1,0:T(8,128)(2,1)S(1)} %pad_maximum_fusion.17), channel_id=1, source_target_pairs={{0,8},{8,0},{16,24},{24,16},{1,9},{9,1},{17,25},{25,17},{2,10},{10... | collective-permute-start | bytes 3244040 | tf_op jit(solution)/shard_map/ppermute | solution.py:241
  643.6 26.2 %collective-permute-start.14 = (bf16[2,528,512]{2,1,0:T(8,128)(2,1)S(1)}, bf16[2,528,512]{2,1,0:T(8,128)(2,1)S(1)}, u32[]{:S(2)}, u32[]{:S(2)}) collective-permute-start(bf16[2,528,512]{2,1,0:T(8,128)(2,1)S(1)} %pad_maximum_fusion.18), channel_id=1, source_target_pairs={{0,16},{8,24},{16,0},{24,8},{1,17},{9,25},{17,1},{25,9},{2,18},{10... | collective-permute-start | bytes 3244040 | tf_op jit(solution)/shard_map/ppermute | solution.py:241
  668.0 13.8 %collective-permute-start.13 = (bf16[1,528,512]{2,1,0:T(8,128)(2,1)S(1)}, bf16[1,528,512]{2,1,0:T(8,128)(2,1)S(1)}, u32[]{:S(2)}, u32[]{:S(2)}) collective-permute-start(bf16[1,528,512]{2,1,0:T(8,128)(2,1)S(1)} %fusion.48), channel_id=1, source_target_pairs={{0,16},{8,24},{16,0},{24,8},{1,17},{9,25},{17,1},{25,9},{2,18},{10... | collective-permute-start | bytes 1622024 | tf_op jit(solution)/shard_map/ppermute | solution.py:241
  682.2 13.0 %collective-permute-start.15 = (bf16[1,528,512]{2,1,0:T(8,128)(2,1)S(1)}, bf16[1,528,512]{2,1,0:T(8,128)(2,1)S(1)}, u32[]{:S(2)}, u32[]{:S(2)}) collective-permute-start(bf16[1,528,512]{2,1,0:T(8,128)(2,1)S(1)} %get-tuple-element.113), channel_id=1, source_target_pairs={{0,8},{8,0},{16,24},{24,16},{1,9},{9,1},{17,25},{25,17},{2,10},{10... | collective-permute-start | bytes 1622024 | tf_op jit(solution)/shard_map/ppermute | solution.py:241
  696.6 11.9 %copy-start.16 = (f32[512,1024]{1,0:T(8,128)S(1)}, f32[512,1024]{1,0:T(8,128)}, u32[]{:S(2)}) copy-start(f32[512,1024]{1,0:T(8,128)} %copy-done.15) | copy-start | bytes 6291460
  696.7 11.8 %copy-start.20 = (bf16[1,512,1024]{2,1,0:T(8,128)(2,1)S(1)}, bf16[1,512,1024]{2,1,0:T(8,128)(2,1)}, u32[]{:S(2)}) copy-start(bf16[1,512,1024]{2,1,0:T(8,128)(2,1)} %param.17) | copy-start | bytes 3145732
  698.1 6.3 collective-permute-start.22
  699.8 8.6 %collective-permute-start.20 = (bf16[984,128]{1,0:T(8,128)(2,1)S(1)}, bf16[984,128]{1,0:T(8,128)(2,1)S(1)}, u32[]{:S(2)}, u32[]{:S(2)}) collective-permute-start(bf16[984,128]{1,0:T(8,128)(2,1)S(1)} %get-tuple-element.163), channel_id=1, source_target_pairs={{0,8},{8,0},{16,24},{24,16},{1,9},{9,1},{17,25},{25,17},{2,10},{10... | collective-permute-start | bytes 755720 | tf_op jit(solution)/shard_map/ppermute | solution.py:241
  704.4 12.4 %collective-permute-start.23 = (bf16[2,984,128]{2,1,0:T(8,128)(2,1)S(1)}, bf16[2,984,128]{2,1,0:T(8,128)(2,1)S(1)}, u32[]{:S(2)}, u32[]{:S(2)}) collective-permute-start(bf16[2,984,128]{2,1,0:T(8,128)(2,1)S(1)} %pad_maximum_fusion.24), channel_id=1, source_target_pairs={{0,8},{8,0},{16,24},{24,16},{1,9},{9,1},{17,25},{25,17},{2,10},{10... | collective-permute-start | bytes 1511432 | tf_op jit(solution)/shard_map/ppermute | solution.py:241
  708.4 9.0 %collective-permute-start.21 = (bf16[2,984,128]{2,1,0:T(8,128)(2,1)S(1)}, bf16[2,984,128]{2,1,0:T(8,128)(2,1)S(1)}, u32[]{:S(2)}, u32[]{:S(2)}) collective-permute-start(bf16[2,984,128]{2,1,0:T(8,128)(2,1)S(1)} %pad_maximum_fusion.23), channel_id=1, source_target_pairs={{0,16},{8,24},{16,0},{24,8},{1,17},{9,25},{17,1},{25,9},{2,18},{10... | collective-permute-start | bytes 1511432 | tf_op jit(solution)/shard_map/ppermute | solution.py:241
  726.6 6.6 collective-permute-start.18
  728.1 5.8 collective-permute-start.16
  733.2 7.6 %collective-permute-start.19 = (bf16[2,528,128]{2,1,0:T(8,128)(2,1)S(1)}, bf16[2,528,128]{2,1,0:T(8,128)(2,1)S(1)}, u32[]{:S(2)}, u32[]{:S(2)}) collective-permute-start(bf16[2,528,128]{2,1,0:T(8,128)(2,1)S(1)} %pad_maximum_fusion.26), channel_id=1, source_target_pairs={{0,8},{8,0},{16,24},{24,16},{1,9},{9,1},{17,25},{25,17},{2,10},{10... | collective-permute-start | bytes 811016 | tf_op jit(solution)/shard_map/ppermute | solution.py:241
  733.9 7.3 collective-permute-start.17
  (34 other events, 79.4 us)
Sparse Core Ops, SparseCore 0:
  63.0 17.8 all-gather.8
  83.0 73.1 all-gather.6
  269.1 7.9 all-gather.10
  303.0 9.1 all-gather.12
  313.6 11.7 all-gather.14
  345.3 10.7 reduce-scatter.7
  358.4 10.7 reduce-scatter.5
  625.5 14.2 reduce-scatter.9
  642.2 43.5 reduce-scatter.13
  696.8 28.7 reduce-scatter.11

commit v3 on v2

--- a/solution.py
+++ b/solution.py
@@ -274,15 +274,20 @@
 def scatter_first(blocks):
     half = blocks.shape[2] // 2
     own = lax.axis_index("dp")
+    routes = ((0, (1, 2)), (half, (2, 1)))
+
+    def block(index, start):
+        return lax.dynamic_slice(blocks, (index ^ own, 0, start), (1, blocks.shape[1], half))
+
+    fars = [
+        swap(jnp.concatenate([block(first, start), block(3, start)]), first)
+        for start, (first, _) in routes
+    ]
+    fars = lax.optimization_barrier(fars)
     sides = []
-    for start, (first, second) in ((0, (1, 2)), (half, (2, 1))):
-        def block(index):
-            return lax.dynamic_slice(
-                blocks, (index ^ own, 0, start), (1, blocks.shape[1], half)
-            )
-        far = swap(jnp.concatenate([block(first), block(3)]), first)
-        near = block(0).astype(F32) + far[:1].astype(F32)
-        passed = (block(second).astype(F32) + far[1:].astype(F32)).astype(BF16)
+    for far, (start, (_, second)) in zip(fars, routes):
+        near = block(0, start).astype(F32) + far[:1].astype(F32)
+        passed = (block(second, start).astype(F32) + far[1:].astype(F32)).astype(BF16)
         sides.append((near, passed))
     return sides
 
@@ -407,8 +412,9 @@
     def finish(owned):
         return gather_dp(lax.psum_scatter(owned, "row", scatter_dimension=1, tiled=True)).astype(F32)
 
-    grad_raw = gather_heads(jnp.concatenate(back, axis=1)).astype(F32)
+    grad_raw = gather_heads(jnp.concatenate(back, axis=1))
     mlp_owned, grad_raw = lax.optimization_barrier((mlp_owned, grad_raw))
+    grad_raw = grad_raw.astype(F32)
     mlp_sums = finish(mlp_owned)
     mlp_sums = [
         mlp_sums[:, index * quarter : (index + 1) * quarter].reshape(hidden, -1) for index in range(3)

time: 760 us -> 746 us (0.982)
  local copies, waits for them, and re-layouts: 105 us -> 93.7 us
    convert_element_type x2 -> x0, local copies, waits for them, and re-layouts: 16.3 us -> none  [body(): grad_raw = gather_heads(jnp.concatenate(back, axis=1)).astype(F32)]
  transfers between devices with their start and end apart: 37 -> 37, of which waited for: 24 -> 25; matrix products, arithmetic and copies ran while one was open for 18% -> 19% of each run, Pallas kernels for 12% -> 12%
where the time goes in v3:
time: 746 us; the launch traced here: 737 us
  waiting for transfers between devices  277 us (37%)
  local copies, waits for them, and re-layouts  93.7 us (13%)
  Pallas kernels  87.8 us (12%)
  matrix products  79 us (11%)
  other arithmetic  76.1 us (10%)
  blocking collectives  61.6 us (8%)
  starting transfers between devices  46.3 us (6%)
  between operations  15.5 us (2%)
    ppermute x24, waiting for transfers between devices, swap(): return lax.ppermute(array, 'dp', pairs)  145 us
    all_to_all x1, waiting for transfers between devices, gather_heads(): moved = lax.all_to_all(packed, 'row', 0, 0, tiled=True)  65.6 us
    pallas_call x1, Pallas kernels, attend_back(): pl.pallas_call(backward_kernel, grid_spec=pltpu.PrefetchScalarGridSpec(nu...  54.9 us
    dot_general x5, matrix products, times_transpose(): lax.dot_general(left_side, right_side, (((1,), (1,)), ((), ())), preferre...  35.7 us
    all_gather x2, blocking collectives, gather(): return lax.all_gather(array, axis, axis=dim, tiled=True)  33.7 us
    all_gather x5, waiting for transfers between devices, gather(): return lax.all_gather(array, axis, axis=dim, tiled=True)  33.7 us
    pallas_call x1, Pallas kernels, attend(): pl.pallas_call(forward_kernel, grid_spec=pltpu.PrefetchScalarGridSpec(num...  32.9 us
    ppermute x24, starting transfers between devices, swap(): return lax.ppermute(array, 'dp', pairs)  30.7 us
  transfers between devices with their start and end apart: 37, of which 25 were waited for; matrix products, arithmetic and copies ran while one was open for 19% of the time, Pallas kernels for 12%

profile of v3, /device:TPU:0, one launch (start us, length us, event | category | flops | bytes accessed | tf_op | source)
XLA Modules:
  0.0 736.8 jit_solution(5466892605746563601)
XLA Ops:
  10.1 21.3 %all_gather.22 = bf16[384,1024]{1,0:T(8,128)(2,1)S(1)} all-gather(bf16[384,256]{1,0:T(8,128)(2,1)S(1)} %bitcast.281), channel_id=1, replica_groups=mesh['dp'=4,'row'=4,'col'=2] {'row'}, dimensions={1}, use_global_device_ids=true | all-gather | bytes 983040 | tf_op jit(solution)/shard_map/all_gather | solution.py:309
  35.5 5.2 collective-permute-done.2
  45.6 13.2 %collective-permute-done.3 = bf16[2,384,512]{2,1,0:T(8,128)(2,1)S(1)} collective-permute-done((bf16[2,384,512]{2,1,0:T(8,128)(2,1)}, bf16[2,384,512]{2,1,0:T(8,128)(2,1)S(1)}, u32[]{:S(2)}, u32[]{:S(2)}) %collective-permute-start.3) | collective-permute-done | bytes 786464 | tf_op jit(solution)/shard_map/ppermute | solution.py:241
  63.8 12.4 %all_gather.21 = s32[1,2048]{1,0:T(1,128)S(1)} all-gather(s32[1,512]{1,0:T(1,128)S(1)} %copy-done.49), channel_id=1, replica_groups=mesh['dp'=4,'row'=4,'col'=2] {'row'}, dimensions={1}, use_global_device_ids=true | all-gather | bytes 10240 | tf_op jit(solution)/shard_map/all_gather | solution.py:309
  83.1 2.9 copy.76
  86.0 8.3 %fusion.54 = f32[512,3072]{1,0:T(8,128)} fusion(bf16[3072,1024]{1,0:T(8,128)(2,1)} %bitcast.289, bf16[1,512,1024]{2,1,0:T(8,128)(2,1)S(1)} %copy-done.17, f32[1024]{0:T(1024)S(1)} %copy-done.45, f32[512]{0:T(512)S(1)} %fusion.67, f32[512]{0:T(512)S(1)} %broadcast_multiply_fusion.1), kind=kOutput, calls=%fused_computation.126 | convolution fusion | flops 3223846912 | bytes 13639680 | tf_op jit(solution)/shard_map/dot_general | solution.py:50
  96.1 8.4 %fusion.74 = (f32[512,992]{1,0:T(8,128)}, f32[512,992]{1,0:T(8,128)}, f32[512,992]{1,0:T(8,128)}, f32[512,992]{1,0:T(8,128)}) fusion(f32[512,3072]{1,0:T(8,128)} %fusion.54), kind=kLoop, calls=%fused_computation.224 | loop fusion | bytes 16252928 | tf_op jit(solution)/shard_map/slice | solution.py:38
  107.8 6.6 fusion.27
  117.3 3.2 pad_maximum_fusion.2
  120.5 4.6 all-to-all-start
  125.5 30.8 %all-gather.7.cloned.1.call-done = bf16[1112,1024]{1,0:T(8,128)(2,1)} async-done(((bf16[1112,256]{1,0:T(8,128)(2,1)}), bf16[1112,1024]{1,0:T(8,128)(2,1)}) %all-gather.7.cloned.1.call-update) | async-done | bytes 2277392 | tf_op jit(solution)/shard_map/all_gather | solution.py:309
  161.3 23.6 %collective-permute-done.5 = bf16[1112,512]{1,0:T(8,128)(2,1)S(1)} collective-permute-done((bf16[1112,512]{1,0:T(8,128)(2,1)S(1)}, bf16[1112,512]{1,0:T(8,128)(2,1)S(1)}, u32[]{:S(2)}, u32[]{:S(2)}) %collective-permute-start.5) | collective-permute-done | bytes 1138720 | tf_op jit(solution)/shard_map/ppermute | solution.py:241
  188.1 12.7 %all-to-all-done = bf16[4,512,768]{1,2,0:T(8,128)(2,1)} async-done(((bf16[4,512,768]{1,2,0:T(8,128)(2,1)}), bf16[4,512,768]{1,2,0:T(8,128)(2,1)}, u32[]{:S(2)}, u32[]{:S(2)}) %all-to-all-start) | async-done | bytes 3145760 | tf_op jit(solution)/shard_map/all_to_all | solution.py:337
  200.8 3.2 copy.83
  210.2 2.3 copy.84.vt_ref
  214.9 32.9 %attend.1 = (bf16[2048,256]{1,0:T(8,128)(2,1)S(1)}, f32[4,2048]{1,0:T(4,128)S(1)}) custom-call(s32[2,8]{1,0:T(2,128)S(1)} %pad_add_fusion.bounds, bf16[2048,768]{1,0:T(8,128)(2,1)S(1)} %bitcast.230, bf16[2048,768]{1,0:T(8,128)(2,1)S(1)} %bitcast.231, bf16[256,2048]{1,0:T(8,128)(2,1)S(1)} %copy-done.6, s32[1,2048]{1,0:T(1,128)S(1)} %all_gather.21, ...), custom_call_target="tpu_custom_call" | custom-call | flops 4294967296 | bytes 4194304 | tf_op jit(solution)/shard_map/attend/pallas_call | solution.py:159
  247.8 7.4 collective-permute-done.6
  259.2 3.9 maximum_maximum_fusion
  263.1 3.1 constant_dynamic-slice_fusion.15
  267.5 2.2 pad_maximum_fusion.19
  270.4 27.8 %all_to_all.42 = bf16[4,512,256]{1,2,0:T(8,128)(2,1)} all-to-all(bf16[4,512,256]{1,2,0:T(8,128)(2,1)S(1)} %copy.86), channel_id=1, replica_groups=mesh['dp'=4,'row'=4,'col'=2] {'row'}, dimensions={0} | all-to-all | bytes 2097152 | tf_op jit(solution)/shard_map/all_to_all | solution.py:341
  298.3 3.6 fusion.85
  305.0 5.9 pad_maximum_fusion.5
  310.9 2.3 all-gather.13.cloned.1.call-done
  313.2 7.8 %fusion.87 = f32[1024,1312]{0,1:T(8,128)} fusion(bf16[1024,1024]{1,0:T(8,128)(2,1)} %all-gather.13.cloned.1.call-done, bf16[1312,1024]{1,0:T(8,128)(2,1)} %bitcast.258), kind=kOutput, calls=%fused_computation.237 | convolution fusion | flops 2751463424 | bytes 10158080 | tf_op jit(solution)/shard_map/dot_general | solution.py:50
  321.0 4.7 fusion.86
  326.3 11.3 %fusion.4 = (bf16[1024,1312]{0,1:T(8,128)(2,1)S(1)}, bf16[1024,1312]{0,1:T(8,128)(2,1)S(1)}, bf16[1024,1312]{0,1:T(8,128)(2,1)}) fusion(f32[1024,1312]{0,1:T(8,128)} %fusion.86, f32[1024,1312]{0,1:T(8,128)} %fusion.87, bf16[1312,1024]{1,0:T(8,128)(2,1)} %bitcast.256, bf16[1,1024,1024]{2,1,0:T(8,128)(2,1)} %all-gather.15.cloned.1.call-done), kind=kOutput, calls=%fused_computation.10 | convolution fusion | flops 2772959232 | bytes 23592960 | tf_op jit(solution)/shard_map/dot_general | solution.py:50
  337.7 3.5 fusion.88
  341.4 4.7 add_convert_fusion
  346.3 7.4 %convolution_convert_fusion.5 = bf16[1024,1024]{1,0:T(8,128)(2,1)} fusion(bf16[1024,1312]{0,1:T(8,128)(2,1)} %get-tuple-element.88, bf16[1312,1024]{1,0:T(8,128)(2,1)} %bitcast.257), kind=kOutput, calls=%fused_computation.104 | convolution fusion | flops 2752512000 | bytes 7471104 | tf_op jit(solution)/shard_map/dot_general | solution.py:56
  353.7 5.6 convolution_convert_fusion.1
  359.4 3.2 convolution_convert_fusion.2
  362.6 3.2 convolution_convert_fusion.3
  375.6 3.4 fusion.72
  384.7 4.8 all-to-all-start.2
  391.1 24.2 %collective-permute-done.8 = bf16[2,984,512]{2,1,0:T(8,128)(2,1)} collective-permute-done((bf16[2,984,512]{2,1,0:T(8,128)(2,1)}, bf16[2,984,512]{2,1,0:T(8,128)(2,1)}, u32[]{:S(2)}, u32[]{:S(2)}) %collective-permute-start.8) | collective-permute-done | bytes 2015264 | tf_op jit(solution)/shard_map/ppermute | solution.py:241
  415.2 2.9 collective-permute-done.9
  418.1 6.5 add_convert_fusion.5
  426.2 2.9 copy.88
  433.5 54.9 %attend_back.1 = (bf16[2048,256]{1,0:T(8,128)(2,1)S(1)}, bf16[2048,256]{1,0:T(8,128)(2,1)S(1)}, bf16[2048,256]{1,0:T(8,128)(2,1)S(1)}) custom-call(s32[2,8]{1,0:T(2,128)S(1)} %pad_add_fusion.bounds, bf16[2048,768]{1,0:T(8,128)(2,1)} %bitcast.232, bf16[2048,256]{1,0:T(8,128)(2,1)S(1)} %bitcast.236, bf16[2048,768]{1,0:T(8,128)(2,1)} %bitcast.233, ...), custom_call_target="tpu_custom_call" | custom-call | flops 10737418240 | bytes 7340032 | tf_op jit(solution)/shard_map/attend_back/pallas_call | solution.py:193
  492.7 2.9 pad_maximum_fusion.3
  495.6 4.7 copy.91
  500.3 4.6 all-to-all-start.3
  504.9 4.2 convolution_convert_fusion.4
  509.0 65.6 %all-to-all-done.3 = bf16[4,512,768]{1,2,0:T(8,128)(2,1)S(1)} async-done(((bf16[4,512,768]{1,2,0:T(8,128)(2,1)}), bf16[4,512,768]{1,2,0:T(8,128)(2,1)S(1)}, u32[]{:S(2)}, u32[]{:S(2)}) %all-to-all-start.3) | async-done | bytes 3145760 | tf_op jit(solution)/shard_map/all_to_all | solution.py:341
  574.7 4.0 copy.92
  578.7 4.7 reshape.470
  587.9 2.5 fusion.35
  590.4 6.7 convolution_convert_fusion
  597.1 3.6 fusion.20
  603.0 3.6 copy.97
  606.7 4.1 fusion.1
  611.7 13.6 %reduce-scatter.10.cloned.1.call-done = bf16[1,4,528,1024]{3,2,1,0:T(8,128)(2,1)} async-done(((bf16[2,4,528,1024]{3,2,1,0:T(8,128)(2,1)}), bf16[1,4,528,1024]{3,2,1,0:T(8,128)(2,1)}) %reduce-scatter.10.cloned.1.call-update) | async-done | bytes 4325392 | tf_op jit(solution)/shard_map/reduce_scatter | solution.py:449
  630.6 22.7 %collective-permute-done.12 = bf16[2,528,512]{2,1,0:T(8,128)(2,1)S(1)} collective-permute-done((bf16[2,528,512]{2,1,0:T(8,128)(2,1)S(1)}, bf16[2,528,512]{2,1,0:T(8,128)(2,1)S(1)}, u32[]{:S(2)}, u32[]{:S(2)}) %collective-permute-start.12) | collective-permute-done | bytes 1081376 | tf_op jit(solution)/shard_map/ppermute | solution.py:241
  656.6 11.9 %collective-permute-done.14 = bf16[1,528,512]{2,1,0:T(8,128)(2,1)S(1)} collective-permute-done((bf16[1,528,512]{2,1,0:T(8,128)(2,1)S(1)}, bf16[1,528,512]{2,1,0:T(8,128)(2,1)S(1)}, u32[]{:S(2)}, u32[]{:S(2)}) %collective-permute-start.14) | collective-permute-done | bytes 540704 | tf_op jit(solution)/shard_map/ppermute | solution.py:241
  669.4 12.2 %collective-permute-done.15 = bf16[1,528,512]{2,1,0:T(8,128)(2,1)S(1)} collective-permute-done((bf16[1,528,512]{2,1,0:T(8,128)(2,1)S(1)}, bf16[1,528,512]{2,1,0:T(8,128)(2,1)S(1)}, u32[]{:S(2)}, u32[]{:S(2)}) %collective-permute-start.15) | collective-permute-done | bytes 540704 | tf_op jit(solution)/shard_map/ppermute | solution.py:241
  686.5 4.2 collective-permute-done.22
  691.4 3.2 collective-permute-done.20
  694.8 3.1 fusion.52
  697.9 5.1 collective-permute-done.23
  704.1 2.3 maximum_convert_fusion
  706.5 4.3 reduce-scatter.12.cloned.1.call-done
  714.8 3.6 fusion.75
  721.9 4.2 collective-permute-done.19
  (283 shorter events, 120.9 us)
Async XLA Ops:
  7.2 78.8 %all-gather.9.cloned.1.call-start = ((), (), s32[]{:S(2)}) async-start(), calls=%async_computation.10 | async-start | bytes 9437184 | tf_op jit(solution)/shard_map/all_gather | solution.py:309
  32.4 8.3 %collective-permute-start.2 = (bf16[384,512]{1,0:T(8,128)(2,1)S(1)}, bf16[384,512]{1,0:T(8,128)(2,1)S(1)}, u32[]{:S(2)}, u32[]{:S(2)}) collective-permute-start(bf16[384,512]{1,0:T(8,128)(2,1)S(1)} %get-tuple-element.164), channel_id=1, source_target_pairs={{0,16},{8,24},{16,0},{24,8},{1,17},{9,25},{17,1},{25,9},{2,18},{10... | collective-permute-start | bytes 1179656 | tf_op jit(solution)/shard_map/ppermute | solution.py:241
  34.0 9.1 %collective-permute-start = (bf16[384,512]{1,0:T(8,128)(2,1)S(1)}, bf16[384,512]{1,0:T(8,128)(2,1)S(1)}, u32[]{:S(2)}, u32[]{:S(2)}) collective-permute-start(bf16[384,512]{1,0:T(8,128)(2,1)S(1)} %get-tuple-element.165), channel_id=1, source_target_pairs={{0,8},{8,0},{16,24},{24,16},{1,9},{9,1},{17,25},{25,17},{2,10},{10... | collective-permute-start | bytes 1179656 | tf_op jit(solution)/shard_map/ppermute | solution.py:241
  41.6 17.1 %collective-permute-start.3 = (bf16[2,384,512]{2,1,0:T(8,128)(2,1)}, bf16[2,384,512]{2,1,0:T(8,128)(2,1)S(1)}, u32[]{:S(2)}, u32[]{:S(2)}) collective-permute-start(bf16[2,384,512]{2,1,0:T(8,128)(2,1)} %pad_maximum_fusion.21), channel_id=1, source_target_pairs={{0,8},{8,0},{16,24},{24,16},{1,9},{9,1},{17,25},{25,17},{2,10},{10... | collective-permute-start | bytes 2359304 | tf_op jit(solution)/shard_map/ppermute | solution.py:241
  44.1 15.6 %collective-permute-start.1 = (bf16[2,384,512]{2,1,0:T(8,128)(2,1)}, bf16[2,384,512]{2,1,0:T(8,128)(2,1)S(1)}, u32[]{:S(2)}, u32[]{:S(2)}) collective-permute-start(bf16[2,384,512]{2,1,0:T(8,128)(2,1)} %pad_maximum_fusion.20), channel_id=1, source_target_pairs={{0,16},{8,24},{16,0},{24,8},{1,17},{9,25},{17,1},{25,9},{2,18},{10... | collective-permute-start | bytes 2359304 | tf_op jit(solution)/shard_map/ppermute | solution.py:241
  62.9 13.3 %copy-start.17 = (bf16[1,512,1024]{2,1,0:T(8,128)(2,1)S(1)}, bf16[1,512,1024]{2,1,0:T(8,128)(2,1)}, u32[]{:S(2)}) copy-start(bf16[1,512,1024]{2,1,0:T(8,128)(2,1)} %param.9) | copy-start | bytes 3145732
  62.9 93.3 %all-gather.7.cloned.1.call-start = ((), (), s32[]{:S(2)}) async-start(), calls=%async_computation.9 | async-start | bytes 2846720 | tf_op jit(solution)/shard_map/all_gather | solution.py:309
  63.7 43.7 %copy-start.47 = (pred[1024]{0:T(1024)(128)(4,1)}, pred[1024]{0:T(1024)(128)(4,1)S(1)}, u32[]{:S(2)}) copy-start(pred[1024]{0:T(1024)(128)(4,1)S(1)} %fusion.66) | copy-start | bytes 3076
  63.7 43.7 %copy-start.35 = (s32[1024]{0:T(1024)}, s32[1024]{0:T(1024)S(1)}, u32[]{:S(2)}) copy-start(s32[1024]{0:T(1024)S(1)} %get-tuple-element.188) | copy-start | bytes 12292
  63.7 43.7 %copy-start.37 = (s32[1024]{0:T(1024)}, s32[1024]{0:T(1024)S(1)}, u32[]{:S(2)}) copy-start(s32[1024]{0:T(1024)S(1)} %get-tuple-element.189) | copy-start | bytes 12292
  76.4 9.6 %copy-start.39 = (f32[512]{0:T(512)}, f32[512]{0:T(512)S(1)}, u32[]{:S(2)}) copy-start(f32[512]{0:T(512)S(1)} %broadcast_multiply_fusion.1) | copy-start | bytes 6148
  77.4 8.5 %copy-start.43 = (f32[512]{0:T(512)}, f32[512]{0:T(512)S(1)}, u32[]{:S(2)}) copy-start(f32[512]{0:T(512)S(1)} %fusion.67) | copy-start | bytes 6148
  81.3 26.2 %copy-start.11 = (f32[512,1024]{1,0:T(8,128)}, f32[512,1024]{1,0:T(8,128)S(1)}, u32[]{:S(2)}) copy-start(f32[512,1024]{1,0:T(8,128)S(1)} %copy.77) | copy-start | bytes 6291460
  120.5 80.3 %all-to-all-start = ((bf16[4,512,768]{1,2,0:T(8,128)(2,1)}), bf16[4,512,768]{1,2,0:T(8,128)(2,1)}, u32[]{:S(2)}, u32[]{:S(2)}) async-start(bf16[4,512,768]{1,2,0:T(8,128)(2,1)} %bitcast.23), calls=%async_computation | async-start | bytes 6291456 | tf_op jit(solution)/shard_map/all_to_all | solution.py:337
  125.1 173.1 %all-gather.11.cloned.1.call-start = ((), (), s32[]{:S(2)}) async-start(), calls=%async_computation.11 | async-start | bytes 3145728 | tf_op jit(solution)/shard_map/all_gather | solution.py:309
  158.3 26.7 %collective-permute-start.5 = (bf16[1112,512]{1,0:T(8,128)(2,1)S(1)}, bf16[1112,512]{1,0:T(8,128)(2,1)S(1)}, u32[]{:S(2)}, u32[]{:S(2)}) collective-permute-start(bf16[1112,512]{1,0:T(8,128)(2,1)S(1)} %get-tuple-element.141), channel_id=1, source_target_pairs={{0,16},{8,24},{16,0},{24,8},{1,17},{9,25},{17,1},{25,9},{2,18},{10... | collective-permute-start | bytes 3416072 | tf_op jit(solution)/shard_map/ppermute | solution.py:241
  159.6 26.9 %collective-permute-start.4 = (bf16[1112,512]{1,0:T(8,128)(2,1)S(1)}, bf16[1112,512]{1,0:T(8,128)(2,1)S(1)}, u32[]{:S(2)}, u32[]{:S(2)}) collective-permute-start(bf16[1112,512]{1,0:T(8,128)(2,1)S(1)} %get-tuple-element.142), channel_id=1, source_target_pairs={{0,8},{8,0},{16,24},{24,16},{1,9},{9,1},{17,25},{25,17},{2,10},{10... | collective-permute-start | bytes 3416072 | tf_op jit(solution)/shard_map/ppermute | solution.py:241
  203.9 8.5 %copy-start.2 = (bf16[4,512,768]{2,1,0:T(8,128)(2,1)}, bf16[4,512,768]{2,1,0:T(8,128)(2,1)S(1)}, u32[]{:S(2)}) copy-start(bf16[4,512,768]{2,1,0:T(8,128)(2,1)S(1)} %copy.83) | copy-start | bytes 9437188
  204.0 51.3 %collective-permute-start.6 = (bf16[2,1112,512]{2,1,0:T(8,128)(2,1)}, bf16[2,1112,512]{2,1,0:T(8,128)(2,1)}, u32[]{:S(2)}, u32[]{:S(2)}) collective-permute-start(bf16[2,1112,512]{2,1,0:T(8,128)(2,1)} %pad_maximum_fusion.11), channel_id=1, source_target_pairs={{0,16},{8,24},{16,0},{24,8},{1,17},{9,25},{17,1},{25,9},{2,18},{10... | collective-permute-start | bytes 6832136 | tf_op jit(solution)/shard_map/ppermute | solution.py:241
  205.5 51.2 %collective-permute-start.7 = (bf16[2,1112,512]{2,1,0:T(8,128)(2,1)}, bf16[2,1112,512]{2,1,0:T(8,128)(2,1)}, u32[]{:S(2)}, u32[]{:S(2)}) collective-permute-start(bf16[2,1112,512]{2,1,0:T(8,128)(2,1)} %pad_maximum_fusion.12), channel_id=1, source_target_pairs={{0,8},{8,0},{16,24},{24,16},{1,9},{9,1},{17,25},{25,17},{2,10},{10... | collective-permute-start | bytes 6832136 | tf_op jit(solution)/shard_map/ppermute | solution.py:241
  214.9 41.7 %copy-start.21 = (bf16[2,1112,512]{2,1,0:T(8,128)(2,1)S(1)}, bf16[2,1112,512]{2,1,0:T(8,128)(2,1)}, u32[]{:S(2)}) copy-start(bf16[2,1112,512]{2,1,0:T(8,128)(2,1)} %pad_maximum_fusion.12) | copy-start | bytes 6832132
  247.8 9.0 %copy-start.3 = (bf16[2048,256]{1,0:T(8,128)(2,1)}, bf16[2048,256]{1,0:T(8,128)(2,1)S(1)}, u32[]{:S(2)}) copy-start(bf16[2048,256]{1,0:T(8,128)(2,1)S(1)} %get-tuple-element.51) | copy-start | bytes 3145732
  269.8 43.3 %all-gather.13.cloned.1.call-start = ((), (), s32[]{:S(2)}) async-start(), calls=%async_computation.12 | async-start | bytes 3145728 | tf_op jit(solution)/shard_map/all_gather | solution.py:309
  303.8 22.5 %all-gather.15.cloned.1.call-start = ((), (), s32[]{:S(2)}) async-start(), calls=%async_computation.18 | async-start | bytes 3145728 | tf_op jit(solution)/shard_map/all_gather | solution.py:309
  304.4 69.0 %reduce-scatter.8.cloned.1.call-start = ((), (), s32[]{:S(2)}) async-start(), calls=%async_computation.14 | async-start | bytes 3145728 | tf_op jit(solution)/shard_map/reduce_scatter | solution.py:386
  313.2 7.8 %copy-start.29 = (bf16[4,328,1024]{2,1,0:T(8,128)(2,1)S(1)}, bf16[4,328,1024]{2,1,0:T(8,128)(2,1)}, u32[]{:S(2)}) copy-start(bf16[4,328,1024]{2,1,0:T(8,128)(2,1)} %get-tuple-element.99) | copy-start | bytes 8060932
  313.2 7.8 %copy-start.51 = (bf16[1024,1024]{1,0:T(8,128)(2,1)S(1)}, bf16[1024,1024]{1,0:T(8,128)(2,1)}, u32[]{:S(2)}) copy-start(bf16[1024,1024]{1,0:T(8,128)(2,1)} %all-gather.13.cloned.1.call-done) | copy-start | bytes 6291460
  326.3 11.3 %copy-start.30 = (bf16[4,328,1024]{2,1,0:T(8,128)(2,1)S(1)}, bf16[4,328,1024]{2,1,0:T(8,128)(2,1)}, u32[]{:S(2)}) copy-start(bf16[4,328,1024]{2,1,0:T(8,128)(2,1)} %get-tuple-element.99) | copy-start | bytes 8060932
  337.6 3.5 copy-start.53
  337.6 3.5 copy-start.55
  337.7 3.7 copy-start.28
  346.1 29.5 %reduce-scatter.6.cloned.1.call-start = ((), (), s32[]{:S(2)}) async-start(), calls=%async_computation.13 | async-start | bytes 3145728 | tf_op jit(solution)/shard_map/reduce_scatter | solution.py:386
  353.7 5.7 copy-start.52
  353.7 5.7 copy-start.56
  366.5 5.5 copy-start.9
  368.8 46.4 %collective-permute-start.8 = (bf16[2,984,512]{2,1,0:T(8,128)(2,1)}, bf16[2,984,512]{2,1,0:T(8,128)(2,1)}, u32[]{:S(2)}, u32[]{:S(2)}) collective-permute-start(bf16[2,984,512]{2,1,0:T(8,128)(2,1)} %pad_maximum_fusion.13), channel_id=1, source_target_pairs={{0,8},{8,0},{16,24},{24,16},{1,9},{9,1},{17,25},{25,17},{2,10},{10... | collective-permute-start | bytes 6045704 | tf_op jit(solution)/shard_map/ppermute | solution.py:241
  372.0 46.1 %collective-permute-start.9 = (bf16[2,984,512]{2,1,0:T(8,128)(2,1)}, bf16[2,984,512]{2,1,0:T(8,128)(2,1)}, u32[]{:S(2)}, u32[]{:S(2)}) collective-permute-start(bf16[2,984,512]{2,1,0:T(8,128)(2,1)} %pad_maximum_fusion.14), channel_id=1, source_target_pairs={{0,16},{8,24},{16,0},{24,8},{1,17},{9,25},{17,1},{25,9},{2,18},{10... | collective-permute-start | bytes 6045704 | tf_op jit(solution)/shard_map/ppermute | solution.py:241
  384.7 39.9 %all-to-all-start.2 = ((bf16[4,512,256]{2,1,0:T(8,128)(2,1)}), bf16[4,512,256]{2,1,0:T(8,128)(2,1)S(1)}, u32[]{:S(2)}, u32[]{:S(2)}) async-start(bf16[4,512,256]{2,1,0:T(8,128)(2,1)} %bitcast.228), calls=%async_computation.4 | async-start | bytes 2097152 | tf_op jit(solution)/shard_map/all_to_all | solution.py:337
  429.1 59.3 %collective-permute-start.10 = (bf16[1,984,512]{2,1,0:T(8,128)(2,1)}, bf16[1,984,512]{2,1,0:T(8,128)(2,1)S(1)}, u32[]{:S(2)}, u32[]{:S(2)}) collective-permute-start(bf16[1,984,512]{2,1,0:T(8,128)(2,1)} %get-tuple-element.59), channel_id=1, source_target_pairs={{0,16},{8,24},{16,0},{24,8},{1,17},{9,25},{17,1},{25,9},{2,18},{10... | collective-permute-start | bytes 3022856 | tf_op jit(solution)/shard_map/ppermute | solution.py:241
  432.3 56.4 %collective-permute-start.11 = (bf16[1,984,512]{2,1,0:T(8,128)(2,1)S(1)}, bf16[1,984,512]{2,1,0:T(8,128)(2,1)S(1)}, u32[]{:S(2)}, u32[]{:S(2)}) collective-permute-start(bf16[1,984,512]{2,1,0:T(8,128)(2,1)S(1)} %copy-done.33), channel_id=1, source_target_pairs={{0,8},{8,0},{16,24},{24,16},{1,9},{9,1},{17,25},{25,17},{2,10},{10... | collective-permute-start | bytes 3022856 | tf_op jit(solution)/shard_map/ppermute | solution.py:241
  433.5 54.9 %copy-start.25 = (f32[1,984,512]{2,1,0:T(8,128)S(1)}, f32[1,984,512]{2,1,0:T(8,128)}, u32[]{:S(2)}) copy-start(f32[1,984,512]{2,1,0:T(8,128)} %get-tuple-element.58) | copy-start | bytes 6045700
  500.3 74.4 %all-to-all-start.3 = ((bf16[4,512,768]{1,2,0:T(8,128)(2,1)}), bf16[4,512,768]{1,2,0:T(8,128)(2,1)S(1)}, u32[]{:S(2)}, u32[]{:S(2)}) async-start(bf16[4,512,768]{1,2,0:T(8,128)(2,1)} %copy.91), calls=%async_computation.5 | async-start | bytes 6291456 | tf_op jit(solution)/shard_map/all_to_all | solution.py:341
  504.9 120.4 %reduce-scatter.10.cloned.1.call-start = ((), (), s32[]{:S(2)}) async-start(), calls=%async_computation.15 | async-start | bytes 12976128 | tf_op jit(solution)/shard_map/reduce_scatter | solution.py:449
  587.8 9.2 %slice-start = ((s8[6291456]{0:T(1024)(128)(4,1)}), s8[2097152]{0:T(1024)(128)(4,1)S(1)}, s32[]{:S(2)}) async-start(s8[6291456]{0:T(1024)(128)(4,1)} %bitcast.290), calls=%async_computation.19 | async-start | bytes 4194304
  590.4 6.7 slice-start.1
  597.1 3.6 copy-start.42
  603.0 3.7 copy-start.31
  610.8 72.2 %reduce-scatter.14.cloned.1.call-start = ((), (), s32[]{:S(2)}) async-start(), calls=%async_computation.17 | async-start | bytes 2519040 | tf_op jit(solution)/shard_map/reduce_scatter | solution.py:413
  611.5 99.3 %reduce-scatter.12.cloned.1.call-start = ((), (), s32[]{:S(2)}) async-start(), calls=%async_computation.16 | async-start | bytes 1351680 | tf_op jit(solution)/shard_map/reduce_scatter | solution.py:413
  627.0 27.9 %copy-start.26 = (bf16[1,4,528,1024]{3,2,1,0:T(8,128)(2,1)S(1)}, bf16[1,4,528,1024]{3,2,1,0:T(8,128)(2,1)}, u32[]{:S(2)}) copy-start(bf16[1,4,528,1024]{3,2,1,0:T(8,128)(2,1)} %reduce-scatter.10.cloned.1.call-done) | copy-start | bytes 12976132
  627.1 26.1 %collective-permute-start.12 = (bf16[2,528,512]{2,1,0:T(8,128)(2,1)S(1)}, bf16[2,528,512]{2,1,0:T(8,128)(2,1)S(1)}, u32[]{:S(2)}, u32[]{:S(2)}) collective-permute-start(bf16[2,528,512]{2,1,0:T(8,128)(2,1)S(1)} %pad_maximum_fusion.17), channel_id=1, source_target_pairs={{0,8},{8,0},{16,24},{24,16},{1,9},{9,1},{17,25},{25,17},{2,10},{10... | collective-permute-start | bytes 3244040 | tf_op jit(solution)/shard_map/ppermute | solution.py:241
  629.0 25.8 %collective-permute-start.13 = (bf16[2,528,512]{2,1,0:T(8,128)(2,1)S(1)}, bf16[2,528,512]{2,1,0:T(8,128)(2,1)S(1)}, u32[]{:S(2)}, u32[]{:S(2)}) collective-permute-start(bf16[2,528,512]{2,1,0:T(8,128)(2,1)S(1)} %pad_maximum_fusion.18), channel_id=1, source_target_pairs={{0,16},{8,24},{16,0},{24,8},{1,17},{9,25},{17,1},{25,9},{2,18},{10... | collective-permute-start | bytes 3244040 | tf_op jit(solution)/shard_map/ppermute | solution.py:241
  655.0 13.5 %collective-permute-start.14 = (bf16[1,528,512]{2,1,0:T(8,128)(2,1)S(1)}, bf16[1,528,512]{2,1,0:T(8,128)(2,1)S(1)}, u32[]{:S(2)}, u32[]{:S(2)}) collective-permute-start(bf16[1,528,512]{2,1,0:T(8,128)(2,1)S(1)} %fusion.48), channel_id=1, source_target_pairs={{0,16},{8,24},{16,0},{24,8},{1,17},{9,25},{17,1},{25,9},{2,18},{10... | collective-permute-start | bytes 1622024 | tf_op jit(solution)/shard_map/ppermute | solution.py:241
  668.9 12.7 %collective-permute-start.15 = (bf16[1,528,512]{2,1,0:T(8,128)(2,1)S(1)}, bf16[1,528,512]{2,1,0:T(8,128)(2,1)S(1)}, u32[]{:S(2)}, u32[]{:S(2)}) collective-permute-start(bf16[1,528,512]{2,1,0:T(8,128)(2,1)S(1)} %get-tuple-element.121), channel_id=1, source_target_pairs={{0,8},{8,0},{16,24},{24,16},{1,9},{9,1},{17,25},{25,17},{2,10},{10... | collective-permute-start | bytes 1622024 | tf_op jit(solution)/shard_map/ppermute | solution.py:241
  683.0 11.8 %copy-start.16 = (f32[512,1024]{1,0:T(8,128)S(1)}, f32[512,1024]{1,0:T(8,128)}, u32[]{:S(2)}) copy-start(f32[512,1024]{1,0:T(8,128)} %copy-done.15) | copy-start | bytes 6291460
  683.0 11.7 %copy-start.20 = (bf16[1,512,1024]{2,1,0:T(8,128)(2,1)S(1)}, bf16[1,512,1024]{2,1,0:T(8,128)(2,1)}, u32[]{:S(2)}) copy-start(bf16[1,512,1024]{2,1,0:T(8,128)(2,1)} %param.17) | copy-start | bytes 3145732
  684.4 6.3 collective-permute-start.22
  685.9 8.7 %collective-permute-start.20 = (bf16[984,128]{1,0:T(8,128)(2,1)S(1)}, bf16[984,128]{1,0:T(8,128)(2,1)S(1)}, u32[]{:S(2)}, u32[]{:S(2)}) collective-permute-start(bf16[984,128]{1,0:T(8,128)(2,1)S(1)} %get-tuple-element.171), channel_id=1, source_target_pairs={{0,8},{8,0},{16,24},{24,16},{1,9},{9,1},{17,25},{25,17},{2,10},{10... | collective-permute-start | bytes 755720 | tf_op jit(solution)/shard_map/ppermute | solution.py:241
  690.8 12.2 %collective-permute-start.23 = (bf16[2,984,128]{2,1,0:T(8,128)(2,1)S(1)}, bf16[2,984,128]{2,1,0:T(8,128)(2,1)S(1)}, u32[]{:S(2)}, u32[]{:S(2)}) collective-permute-start(bf16[2,984,128]{2,1,0:T(8,128)(2,1)S(1)} %pad_maximum_fusion.24), channel_id=1, source_target_pairs={{0,8},{8,0},{16,24},{24,16},{1,9},{9,1},{17,25},{25,17},{2,10},{10... | collective-permute-start | bytes 1511432 | tf_op jit(solution)/shard_map/ppermute | solution.py:241
  694.7 9.0 %collective-permute-start.21 = (bf16[2,984,128]{2,1,0:T(8,128)(2,1)S(1)}, bf16[2,984,128]{2,1,0:T(8,128)(2,1)S(1)}, u32[]{:S(2)}, u32[]{:S(2)}) collective-permute-start(bf16[2,984,128]{2,1,0:T(8,128)(2,1)S(1)} %pad_maximum_fusion.23), channel_id=1, source_target_pairs={{0,16},{8,24},{16,0},{24,8},{1,17},{9,25},{17,1},{25,9},{2,18},{10... | collective-permute-start | bytes 1511432 | tf_op jit(solution)/shard_map/ppermute | solution.py:241
  711.8 6.6 collective-permute-start.18
  713.4 5.8 collective-permute-start.16
  718.5 7.6 %collective-permute-start.19 = (bf16[2,528,128]{2,1,0:T(8,128)(2,1)S(1)}, bf16[2,528,128]{2,1,0:T(8,128)(2,1)S(1)}, u32[]{:S(2)}, u32[]{:S(2)}) collective-permute-start(bf16[2,528,128]{2,1,0:T(8,128)(2,1)S(1)} %pad_maximum_fusion.26), channel_id=1, source_target_pairs={{0,8},{8,0},{16,24},{24,16},{1,9},{9,1},{17,25},{25,17},{2,10},{10... | collective-permute-start | bytes 811016 | tf_op jit(solution)/shard_map/ppermute | solution.py:241
  719.2 7.3 collective-permute-start.17
  (32 other events, 67.0 us)
Sparse Core Ops, SparseCore 0:
  63.0 17.8 all-gather.8
  83.1 73.1 all-gather.6
  269.9 7.9 all-gather.10
  304.0 9.1 all-gather.12
  314.5 11.7 all-gather.14
  346.2 10.7 reduce-scatter.7
  359.3 10.8 reduce-scatter.5
  610.9 14.3 reduce-scatter.9
  627.6 43.5 reduce-scatter.13
  683.1 27.6 reduce-scatter.11
